TPU v7x, 256 devices: a whole 4x4x8 slice. The times are simulated.
256 devices in a mesh: wide: 32 (over x, y, core), narrow: 8 (over z).
Axes of the slice: x: 4, y: 4, z: 8, core: 2. Of those that a mesh axis runs over, the one named last changes fastest.
Arguments:
- pair_tokens: bfloat16 [256, 2, 128, 768], P(('wide', 'narrow')), may hold values from -6 to 6
- expert_ids: int32 [256, 256, 2], P(('wide', 'narrow')), may hold values from 0 to 31, all different within a row; in each aligned block of 256 rows (0 to 255, 256 to 511, ..., all dimensions but the last counted through in order) at most 17 rows name the same one
- positive: int32 [256], replicated, may hold values from 0 to 255, each once
- w_qkv: bfloat16 [768, 2304], replicated, may hold values from -0.21875 to 0.21875
- w_out: bfloat16 [768, 768], replicated, may hold values from -0.21875 to 0.21875
- w_router: bfloat16 [768, 32], replicated, may hold values from -0.21875 to 0.21875
- w_up: bfloat16 [32, 768, 3072], P('wide', None, 'narrow'), may hold values from -0.21875 to 0.21875
- w_down: bfloat16 [32, 3072, 768], P('wide', 'narrow'), may hold values from -0.109375 to 0.109375
Outputs:
- grad_up: float32 [32, 768, 3072], P('wide', None, 'narrow')
- grad_down: float32 [32, 3072, 768], P('wide', 'narrow')
Inputs may be any that keep to these rules, and one draw needn't show every extreme that they name: `expert_ids`: the two experts of a token differ. Among the 256 tokens of one device no expert is named more than 17 times, and in every draw some device names some expert exactly 17 times. Each document is the positive of exactly one query.
All inputs are finite; a program needn't handle non-finite values.
Results may differ from a plain program's by a relative error of at most 0.023.
Values may be sent and summed in bfloat16 or wider, within the bound.
A program may use at most 128 MiB of HBM per device.

v0:
```python
import math

import jax
import jax.numpy as jnp
from jax import lax
from jax.sharding import PartitionSpec as P

HEADS = 12
HEAD_DIM = 64
SEQ = 128


epsilon = 1e-06
inverse_softmax_warmth = 20.0
loss_scale = 64.0


def rms_scaled(values):
    return values * lax.rsqrt(jnp.mean(values * values, axis=-1, keepdims=True) + epsilon)


def attention_block(tokens, w_qkv, w_out):
    count = tokens.shape[0]
    width = tokens.shape[1]
    normed = rms_scaled(tokens.astype(jnp.float32)).astype(jnp.bfloat16)
    project = jnp.dot(normed, w_qkv, preferred_element_type=jnp.float32)
    project = project.reshape(count // SEQ, SEQ, 3, HEADS, HEAD_DIM)
    query = rms_scaled(project[:, :, 0]).astype(jnp.bfloat16)
    keys_normed = rms_scaled(project[:, :, 1]).astype(jnp.bfloat16)
    values_cast = project[:, :, 2].astype(jnp.bfloat16)
    cosine_logit_matrix = jnp.einsum(
        "sqhe,skhe->shqk", query, keys_normed, preferred_element_type=jnp.float32
    ) / math.sqrt(HEAD_DIM)
    weights = jnp.exp(cosine_logit_matrix)
    weights = (weights / jnp.sum(weights, axis=-1, keepdims=True)).astype(jnp.bfloat16)
    mixed = jnp.einsum("shqk,skhe->sqhe", weights, values_cast, preferred_element_type=jnp.float32)
    mixed = mixed.astype(jnp.bfloat16).reshape(count, width)
    update = jnp.dot(mixed, w_out, preferred_element_type=jnp.float32)
    return (tokens.astype(jnp.float32) + update).astype(jnp.bfloat16)


def gate_pair(logits, picks):
    experts = logits.shape[-1]
    onehot = (picks[:, :, None] == jnp.arange(experts, dtype=jnp.int32)[None, None, :]).astype(
        jnp.float32
    )
    chosen_logits = jnp.sum(onehot * logits[:, None, :], axis=-1)
    first = jax.nn.sigmoid(chosen_logits[:, 0] - chosen_logits[:, 1])
    return jnp.stack([first, 1.0 - first], axis=1)


def slot_positions(picks, experts, capacity):
    flat = picks.reshape(-1)
    onehot = (flat[:, None] == jnp.arange(experts, dtype=jnp.int32)[None, :]).astype(jnp.int32)
    earlier = jnp.cumsum(onehot, axis=0) - onehot
    return flat * capacity + jnp.sum(earlier * onehot, axis=1)


def contract_rows(left, right):
    return lax.dot_general(
        left, right, (((0,), (0,)), ((), ())), preferred_element_type=jnp.float32
    )


def body(pair_tokens, expert_ids, positive, w_qkv, w_out, w_router, w_up, w_down):
    experts = lax.axis_size("wide")
    groups = lax.axis_size("narrow")
    pair_count = pair_tokens.shape[0]
    width = pair_tokens.shape[-1]
    tokens = pair_tokens.reshape(-1, width)
    count = tokens.shape[0]
    capacity = 17 * count // (8 * experts)
    picks = expert_ids.reshape(-1, 2)
    hidden_state = attention_block(tokens, w_qkv, w_out)
    normed = rms_scaled(hidden_state.astype(jnp.float32)).astype(jnp.bfloat16)
    logits = jnp.dot(normed, w_router, preferred_element_type=jnp.float32)
    gates = gate_pair(logits, picks)
    destination = slot_positions(picks, experts, capacity)
    outgoing = jnp.zeros((experts * capacity, width), jnp.bfloat16)
    outgoing = (
        outgoing.at[destination]
        .set(jnp.repeat(normed, 2, axis=0))
        .reshape(experts, capacity, width)
    )
    arrived = lax.all_to_all(outgoing, "wide", split_axis=0, concat_axis=0, tiled=True)
    up_local = w_up[0]
    down_local = w_down[0]
    slot_rows = lax.all_gather(arrived, "narrow", axis=0, tiled=True).reshape(-1, width)
    pre_act = jnp.dot(slot_rows, up_local, preferred_element_type=jnp.float32)
    activated = jax.nn.gelu(pre_act).astype(jnp.bfloat16)
    partial_value = jnp.dot(activated, down_local, preferred_element_type=jnp.float32)
    partial_value = partial_value.reshape(groups, experts * capacity, width)
    summed = lax.psum_scatter(
        partial_value.astype(jnp.bfloat16), "narrow", scatter_dimension=0, tiled=True
    )
    expert_out = summed.reshape(experts, capacity, width)
    returned = lax.all_to_all(expert_out, "wide", split_axis=0, concat_axis=0, tiled=True).reshape(
        experts * capacity, width
    )
    picked = returned[destination].reshape(count, 2, width)
    mixed = hidden_state.astype(jnp.float32) + jnp.sum(
        gates[:, :, None] * picked.astype(jnp.float32), axis=1
    )
    pooled = jnp.mean(mixed.reshape(pair_count, 2, SEQ, width), axis=2)
    length = jnp.sqrt(jnp.sum(pooled * pooled, axis=-1, keepdims=True) + epsilon)
    unit = pooled / length
    search_unit_vector = unit[:, 0]
    passage_unit_vector = unit[:, 1]
    start = lax.axis_index(("wide", "narrow")) * pair_count
    largest_score = lax.Precision.HIGHEST
    gathered_documents = lax.all_gather(passage_unit_vector, ("wide", "narrow"), axis=0, tiled=True)
    cosine_logit_matrix = (
        jnp.dot(search_unit_vector, gathered_documents.T, precision=largest_score)
        * inverse_softmax_warmth
    )
    probs = jnp.exp(cosine_logit_matrix)
    probs = probs / jnp.sum(probs, axis=1, keepdims=True)
    own_positive = lax.dynamic_slice_in_dim(positive, start, pair_count)
    target = (
        own_positive[:, None] == jnp.arange(gathered_documents.shape[0], dtype=jnp.int32)[None, :]
    ).astype(jnp.float32)
    logit_excess_matrix = (probs - target) * loss_scale
    search_embedding_adjoint = (
        jnp.dot(logit_excess_matrix, gathered_documents, precision=largest_score)
        * inverse_softmax_warmth
    )
    document_partials = (
        jnp.dot(logit_excess_matrix.T, search_unit_vector, precision=largest_score)
        * inverse_softmax_warmth
    )
    passage_embedding_adjoint = lax.psum_scatter(
        document_partials, ("wide", "narrow"), scatter_dimension=0, tiled=True
    )
    unit_grad = jnp.stack([search_embedding_adjoint, passage_embedding_adjoint], axis=1)
    pooled_grad = (unit_grad - unit * jnp.sum(unit * unit_grad, axis=-1, keepdims=True)) / length
    token_grad = jnp.broadcast_to(
        (pooled_grad / SEQ)[:, :, None, :], (pair_count, 2, SEQ, width)
    ).reshape(count, width)
    cotangent = (
        (gates[:, :, None] * token_grad[:, None, :]).astype(jnp.bfloat16).reshape(2 * count, width)
    )
    outgoing_grad = jnp.zeros((experts * capacity, width), jnp.bfloat16)
    outgoing_grad = outgoing_grad.at[destination].set(cotangent).reshape(experts, capacity, width)
    arrived_grad = lax.all_to_all(outgoing_grad, "wide", split_axis=0, concat_axis=0, tiled=True)
    grad_rows = lax.all_gather(arrived_grad, "narrow", axis=0, tiled=True).reshape(-1, width)
    down_grad = contract_rows(activated, grad_rows)
    act_grad = jnp.dot(grad_rows, down_local.T, preferred_element_type=jnp.float32)
    unused, pullback = jax.vjp(jax.nn.gelu, pre_act)
    pre_grad = pullback(act_grad)[0].astype(jnp.bfloat16)
    up_grad = contract_rows(slot_rows, pre_grad)
    return (up_grad[None], down_grad[None])


def solution(mesh):
    return jax.shard_map(
        body,
        mesh=mesh,
        in_specs=(
            P(("wide", "narrow"), None, None, None),
            P(("wide", "narrow"), None, None),
            P(),
            P(),
            P(),
            P(),
            P("wide", None, "narrow"),
            P("wide", "narrow", None),
        ),
        out_specs=(P("wide", None, "narrow"), P("wide", "narrow", None)),
        check_vma=False,
    )
```

profile of v0, /device:TPU:1, one launch (start us, length us, event | category | flops | bytes accessed | tf_op | source)
XLA Modules:
  0.0 783.6 jit_solution(5848393974360310661)
XLA Ops:
  12.0 5.8 copy.42
  17.8 3.3 fusion.36
  23.0 3.0 fusion.14
  30.9 3.4 scatter_custom_fusion
  34.6 27.3 %all_to_all.15 = bf16[32,17,768]{2,1,0:T(8,128)(2,1)S(1)} all-to-all(bf16[32,17,768]{2,1,0:T(8,128)(2,1)S(1)} %reshape.360), channel_id=1, replica_groups=mesh['wide'=32,'narrow'=8] {'wide'}, dimensions={0} | all-to-all | bytes 1671168 | tf_op jit(solution)/shard_map/all_to_all | solution.py:85
  63.3 77.0 %all-gather.4.cloned.1.call-done = bf16[256,17,768]{2,0,1:T(8,128)(2,1)} async-done(((bf16[32,17,768]{2,0,1:T(8,128)(2,1)}), bf16[256,17,768]{2,0,1:T(8,128)(2,1)}) %all-gather.4.cloned.1.call-update) | async-done | bytes 6684688 | tf_op jit(solution)/shard_map/all_gather | solution.py:88
  140.3 10.5 %copy.46 = bf16[256,17,768]{2,1,0:T(8,128)(2,1)} copy(bf16[256,17,768]{2,0,1:T(8,128)(2,1)} %all-gather.4.cloned.1.call-done) | data formatting | bytes 13369344 | tf_op jit(solution)/shard_map/all_gather | solution.py:88
  150.8 11.3 %reshape.361 = bf16[4352,768]{1,0:T(8,128)(2,1)} reshape(bf16[256,17,768]{2,1,0:T(8,128)(2,1)} %copy.46) | data formatting | bytes 13369344 | tf_op jit(solution)/shard_map/reshape | solution.py:88
  162.2 10.5 %multiply_convert_fusion = (bf16[4352,384]{1,0:T(8,128)(2,1)S(1)}, f32[4352,384]{1,0:T(8,128)}) fusion(bf16[4352,768]{1,0:T(8,128)(2,1)} %reshape.361, bf16[1,768,384]{2,1,0:T(8,128)(2,1)S(1)} %copy-done.8), kind=kOutput, calls=%fused_computation.12 | convolution fusion | flops 2581954560 | bytes 17301504 | tf_op jit(solution)/shard_map/dot_general | solution.py:89
  174.4 5.6 convolution_convert_fusion
  180.0 77.7 %reduce-scatter.2.cloned.1.call-done = bf16[1,544,768]{2,1,0:T(8,128)(2,1)} async-done(((bf16[8,544,768]{2,1,0:T(8,128)(2,1)}), bf16[1,544,768]{2,1,0:T(8,128)(2,1)}) %reduce-scatter.2.cloned.1.call-update) | async-done | bytes 835600 | tf_op jit(solution)/shard_map/reduce_scatter | solution.py:93
  260.0 7.5 all-to-all-start.1
  269.0 16.8 %all-to-all-done.1 = bf16[32,17,768]{2,1,0:T(8,128)(2,1)S(1)} async-done(((bf16[32,17,768]{2,1,0:T(8,128)(2,1)}), bf16[32,17,768]{2,1,0:T(8,128)(2,1)S(1)}, u32[]{:S(2)}, u32[]{:S(2)}) %all-to-all-start.1) | async-done | bytes 835616 | tf_op jit(solution)/shard_map/all_to_all | solution.py:97
  286.1 2.7 gather_fusion
  293.2 69.7 %all-gather = f32[256,1,768]{2,1,0:T(1,128)S(1)} all-gather(f32[1,1,768]{2,1,0:T(1,128)S(1)} %get-tuple-element.6), channel_id=2, replica_groups=mesh['wide'=32,'narrow'=8] {'wide','narrow'}, dimensions={0}, use_global_device_ids=true | all-gather | bytes 789504 | tf_op jit(solution)/shard_map/all_gather | solution.py:111
  367.3 250.2 %all-reduce.3.cloned.1.call-done = f32[256,768]{1,0:T(8,128)} async-done(((f32[256,768]{1,0:T(8,128)}), f32[256,768]{1,0:T(8,128)}) %all-reduce.3.cloned.1.call-update) | async-done | bytes 786448
  621.1 2.4 mul.254
  623.4 3.6 scatter_custom_fusion.1
  628.5 27.4 %all_to_all.16 = bf16[32,17,768]{2,1,0:T(8,128)(2,1)S(1)} all-to-all(bf16[32,17,768]{2,1,0:T(8,128)(2,1)S(1)} %reshape.366), channel_id=1, replica_groups=mesh['wide'=32,'narrow'=8] {'wide'}, dimensions={0} | all-to-all | bytes 1671168 | tf_op jit(solution)/shard_map/all_to_all | solution.py:144
  657.0 73.8 %all-gather.6.cloned.1.call-done = bf16[256,17,768]{2,0,1:T(8,128)(2,1)} async-done(((bf16[32,17,768]{2,0,1:T(8,128)(2,1)}), bf16[256,17,768]{2,0,1:T(8,128)(2,1)}) %all-gather.6.cloned.1.call-update) | async-done | bytes 6684688 | tf_op jit(solution)/shard_map/all_gather | solution.py:145
  730.8 10.5 %copy.50 = bf16[256,17,768]{2,1,0:T(8,128)(2,1)} copy(bf16[256,17,768]{2,0,1:T(8,128)(2,1)} %all-gather.6.cloned.1.call-done) | data formatting | bytes 13369344 | tf_op jit(solution)/shard_map/all_gather | solution.py:145
  741.3 10.8 %reshape.367 = bf16[4352,768]{1,0:T(8,128)(2,1)} reshape(bf16[256,17,768]{2,1,0:T(8,128)(2,1)} %copy.50) | data formatting | bytes 13369344 | tf_op jit(solution)/shard_map/reshape | solution.py:145
  752.1 7.8 convolution_bitcast_fusion
  759.9 17.0 %fusion.9 = f32[1,768,384]{2,1,0:T(8,128)} fusion(bf16[4352,768]{1,0:T(8,128)(2,1)} %reshape.361, f32[4352,384]{1,0:T(8,128)} %get-tuple-element.11, bf16[4352,768]{1,0:T(8,128)(2,1)} %reshape.367, bf16[1,384,768]{2,1,0:T(8,128)(2,1)S(1)} %copy-done.10), kind=kOutput, calls=%fused_computation.19 | convolution fusion | flops 5167251456 | bytes 21823488 | tf_op jit(solution)/shard_map/dot_general | solution.py:60
  (92 shorter events, 33.7 us)
Async XLA Ops:
  7.2 20.3 %copy-start = (bf16[768,768]{1,0:T(8,128)(2,1)S(1)}, bf16[768,768]{1,0:T(8,128)(2,1)}, u32[]{:S(2)}) copy-start(bf16[768,768]{1,0:T(8,128)(2,1)} %param.12) | copy-start | bytes 3538948
  7.2 133.1 %all-gather.4.cloned.1.call-start = ((), (), s32[]{:S(2)}) async-start(), calls=%async_computation.4 | async-start | bytes 7520256 | tf_op jit(solution)/shard_map/all_gather | solution.py:88
  11.7 6.0 copy-start.3
  12.0 9.1 %copy-start.7 = (s32[32,5]{0,1:T(8,128)}, s32[32,5]{0,1:T(8,128)S(1)}, u32[]{:S(2)}) copy-start(s32[32,5]{0,1:T(8,128)S(1)} %reduce-window.9) | copy-start | bytes 1924
  23.0 7.8 slice-start
  26.0 4.8 copy-start.4
  63.0 194.6 %reduce-scatter.2.cloned.1.call-start = ((), (), s32[]{:S(2)}) async-start(), calls=%async_computation.5 | async-start | bytes 7520256 | tf_op jit(solution)/shard_map/reduce_scatter | solution.py:93
  150.8 11.3 %copy-start.8 = (bf16[1,768,384]{2,1,0:T(8,128)(2,1)S(1)}, bf16[1,768,384]{2,1,0:T(8,128)(2,1)}, u32[]{:S(2)}) copy-start(bf16[1,768,384]{2,1,0:T(8,128)(2,1)} %param.14) | copy-start | bytes 1769476
  162.2 12.2 %copy-start.9 = (bf16[1,384,768]{2,1,0:T(8,128)(2,1)S(1)}, bf16[1,384,768]{2,1,0:T(8,128)(2,1)}, u32[]{:S(2)}) copy-start(bf16[1,384,768]{2,1,0:T(8,128)(2,1)} %param.15) | copy-start | bytes 1769476
  172.7 1.7 copy-start.2
  179.9 88.0 %copy-start.5 = (bf16[768,32]{0,1:T(8,128)(2,1)S(1)}, bf16[768,32]{0,1:T(8,128)(2,1)}, u32[]{:S(2)}) copy-start(bf16[768,32]{0,1:T(8,128)(2,1)} %param.13) | copy-start | bytes 147460
  179.9 88.2 %copy-start.6 = (s32[1,256,2]{1,2,0:T(2,128)S(1)}, s32[1,256,2]{1,2,0:T(2,128)}, u32[]{:S(2)}) copy-start(s32[1,256,2]{1,2,0:T(2,128)} %param.9) | copy-start | bytes 6148
  179.9 88.4 %copy-start.11 = (s32[256]{0:T(256)S(1)}, s32[256]{0:T(256)}, u32[]{:S(2)}) copy-start(s32[256]{0:T(256)} %param.10) | copy-start | bytes 3076
  260.0 25.8 %all-to-all-start.1 = ((bf16[32,17,768]{2,1,0:T(8,128)(2,1)}), bf16[32,17,768]{2,1,0:T(8,128)(2,1)S(1)}, u32[]{:S(2)}, u32[]{:S(2)}) async-start(bf16[32,17,768]{2,1,0:T(8,128)(2,1)} %reshape.362), calls=%async_computation.2 | async-start | bytes 2359296 | tf_op jit(solution)/shard_map/all_to_all | solution.py:97
  267.4 350.1 %all-reduce.3.cloned.1.call-start = ((), (), s32[]{:S(2)}) async-start(), calls=%async_computation.7 | async-start | bytes 1572864
  366.6 364.2 %all-gather.6.cloned.1.call-start = ((), (), s32[]{:S(2)}) async-start(), calls=%async_computation.6 | async-start | bytes 7520256 | tf_op jit(solution)/shard_map/all_gather | solution.py:145
  752.1 7.8 copy-start.10
  759.9 17.0 %copy-start.1 = (bf16[768,768]{1,0:T(8,128)(2,1)S(1)}, bf16[768,768]{1,0:T(8,128)(2,1)}, u32[]{:S(2)}) copy-start(bf16[768,768]{1,0:T(8,128)(2,1)} %param.12) | copy-start | bytes 3538948
Sparse Core Ops, SparseCore 0:
  63.2 77.0 all-gather.3
  180.1 77.5 reduce-scatter.1
  366.7 250.7 all-reduce.2
  657.1 73.6 all-gather.5
where the time goes:
time: 791 us; the launch traced here: 784 us
  waiting for transfers between devices  496 us (63%)
  blocking collectives  124 us (16%)
  local copies, waits for them, and re-layouts  76.6 us (10%)
  matrix products  51.8 us (7%)
  between operations  14.3 us (2%)
  other arithmetic  12.8 us (2%)
  starting transfers between devices  8.23 us (1%)
    unnamed x5, waiting for transfers between devices  250 us
    reduce_scatter x1, waiting for transfers between devices, body(): lax.psum_scatter(partial_value.astype(jnp.bfloat16), 'narrow', scatter_di...  77.7 us
    all_gather x1, waiting for transfers between devices, body(): lax.all_gather(arrived, 'narrow', axis=0, tiled=True).reshape(-1, width)  77 us
    all_gather x1, waiting for transfers between devices, body(): lax.all_gather(arrived_grad, 'narrow', axis=0, tiled=True)  73.8 us
    all_gather x1, blocking collectives, body(): lax.all_gather(passage_unit_vector, ('wide', 'narrow'), axis=0, tiled=True)  69.7 us
    all_to_all x1, blocking collectives, body(): lax.all_to_all(outgoing_grad, 'wide', split_axis=0, concat_axis=0, tiled=...  27.4 us
    all_to_all x1, blocking collectives, body(): lax.all_to_all(outgoing, 'wide', split_axis=0, concat_axis=0, tiled=True)  27.3 us
    dot_general x2, matrix products, contract_rows(): lax.dot_general(left, right, (((0,), (0,)), ((), ())), preferred_element_...  24.8 us
  transfers between devices with their start and end apart: 5, of which 5 were waited for; matrix products, arithmetic and copies ran while one was open for 0% of the time, Pallas kernels for 0%

commit v1 on v0

v1 whole, which is shorter than its diff:
```python
import functools

import jax
import jax.numpy as jnp
from jax import lax
from jax.experimental import pallas as pl
from jax.experimental.pallas import tpu as pltpu
from jax.sharding import PartitionSpec as P

D = 768
FB = 384
SEQ = 128
TOK = 256
NE = 32
MAIN = 16
CHUNKS = 4
EPS = 1e-06
WARMTH = 20.0
LOSS_SCALE = 64.0
VMEM_BYTES = 56 * 2**20
MESH = pl.DeviceIdType.MESH
HIGHEST = lax.Precision.HIGHEST
F32, BF16, I32 = jnp.float32, jnp.bfloat16, jnp.int32


def mm(a, b, ca=1, cb=0, precision=None):
    return lax.dot_general(
        a, b, (((ca,), (cb,)), ((), ())), precision=precision, preferred_element_type=F32
    )


def iota(shape, axis):
    return lax.broadcasted_iota(I32, shape, axis)


def onehot(condition):
    return jnp.where(condition, 1.0, 0.0).astype(BF16)


def rms(v):
    return v * lax.rsqrt(jnp.mean(v * v, axis=-1, keepdims=True) + EPS)


def front_kernel(x_ref, ids_ref, wqkv_ref, wout_ref, wr_ref, main_ref, side_ref, mean_ref, mixed):
    normed = rms(x_ref[...].astype(F32)).astype(BF16)
    wide = 256
    same_head = onehot(iota((wide, wide), 0) // 64 == iota((wide, wide), 1) // 64)
    low = iota((SEQ, 128), 1) < 64
    ones = jnp.ones((SEQ, 128), BF16)

    def head_rms(v):
        square = v * v
        high = square.astype(BF16)
        rest = (square - high.astype(F32)).astype(BF16)
        mean = (mm(high, same_head) + mm(rest, same_head)) * (1.0 / 64.0)
        return (v * lax.rsqrt(mean + EPS)).astype(BF16)

    for block in range(D // wide):
        at = block * wide
        q = head_rms(mm(normed, wqkv_ref[:, at : at + wide]))
        k = head_rms(mm(normed, wqkv_ref[:, D + at : D + at + wide]))
        v = mm(normed, wqkv_ref[:, 2 * D + at : 2 * D + at + wide]).astype(BF16)
        for s in range(TOK // SEQ):
            rows = slice(s * SEQ, (s + 1) * SEQ)
            for c in range(wide // 128):
                lanes = slice(c * 128, (c + 1) * 128)
                qc, kc = q[rows, lanes], k[rows, lanes]
                values = jnp.concatenate([v[rows, lanes], ones], axis=1)
                heads = []
                for half in range(2):
                    qh = jnp.where(low if half == 0 else ~low, qc, jnp.zeros_like(qc))
                    weights = jnp.exp(mm(qh, kc, 1, 1) * 0.125).astype(BF16)
                    both = mm(weights, values)
                    heads.append(both[:, :128] / both[:, 128:])
                mixed[rows, at + c * 128 : at + (c + 1) * 128] = jnp.where(
                    low, heads[0], heads[1]
                ).astype(BF16)

    h = (x_ref[...].astype(F32) + mm(mixed[...], wout_ref[...])).astype(BF16).astype(F32)
    mean_q = jnp.mean(h[:SEQ], axis=0, keepdims=True)
    mean_d = jnp.mean(h[SEQ:], axis=0, keepdims=True)
    mean_ref[...] = jnp.where(
        iota((8, D), 0) == 0, mean_q, jnp.where(iota((8, D), 0) == 1, mean_d, 0.0)
    )
    z = rms(h).astype(BF16)

    logits = mm(wr_ref[...], z, 0, 1)
    names = iota((TOK, NE), 1)
    named = onehot((ids_ref[:, 0:1] == names) | (ids_ref[:, 1:2] == names))
    row, col = iota((TOK, TOK), 0), iota((TOK, TOK), 1)
    picked = mm(named, jnp.concatenate([onehot(row == col), onehot(row < col)], axis=1), 0, 0)
    here = picked[:, :TOK] > 0.5
    rank = jnp.where(here, picked[:, TOK:], -1.0)
    both_logits = jnp.sum(jnp.where(here, logits, 0.0), axis=0, keepdims=True)
    gate = jnp.where(here, 1.0 / (1.0 + jnp.exp(both_logits - 2.0 * logits)), 0.0)

    spread = onehot(iota((NE * MAIN, NE), 0) // MAIN == iota((NE * MAIN, NE), 1))
    slot = (iota((NE * MAIN, TOK), 0) % MAIN).astype(F32)
    main_ref[...] = mm(onehot(mm(spread, rank.astype(BF16)) == slot), z).astype(BF16)

    extra = mm(onehot(rank == float(MAIN)), z).astype(BF16)
    lane = iota((NE, 128), 1)
    gates_q = jnp.zeros((NE, 128), F32)
    gates_d = jnp.zeros((NE, 128), F32)
    for s in range(MAIN + 1):
        chosen = jnp.where(rank == float(s), gate, 0.0)
        gates_q = jnp.where(lane == s, jnp.sum(chosen[:, :SEQ], axis=1, keepdims=True), gates_q)
        gates_d = jnp.where(lane == s, jnp.sum(chosen[:, SEQ:], axis=1, keepdims=True), gates_d)
    parts = [extra[:, c * 128 : (c + 1) * 128] for c in range(D // 128)]
    stacked = jnp.concatenate(parts + [gates_q.astype(BF16), gates_d.astype(BF16)], axis=0)
    r, c = iota((8 * NE, 8 * NE), 0), iota((8 * NE, 8 * NE), 1)
    side_ref[...] = mm(onehot(r == (c % NE) * 8 + c // NE), stacked)


def front(tokens, ids, w_qkv, w_out, w_router):
    return pl.pallas_call(
        front_kernel,
        out_shape=(
            jax.ShapeDtypeStruct((NE * MAIN, D), BF16),
            jax.ShapeDtypeStruct((8 * NE, 128), F32),
            jax.ShapeDtypeStruct((8, D), F32),
        ),
        scratch_shapes=[pltpu.VMEM((TOK, D), BF16)],
        compiler_params=pltpu.CompilerParams(vmem_limit_bytes=VMEM_BYTES),
        name="attention_and_slots",
    )(tokens, ids, w_qkv, w_out, w_router)


def dispatch_kernel(nw, nz, main_ref, side_ref, omain, oside, s1, r1, s2, r2):
    w, z = lax.axis_index("wide"), lax.axis_index("narrow")
    right, left = lax.rem(z + 1, nz), lax.rem(z + nz - 1, nz)
    hops, size = nz // 2, nw // CHUNKS

    barrier = pltpu.get_barrier_semaphore()

    def greet(d, carry):
        pl.semaphore_signal(
            barrier, inc=1, device_id=(lax.rem(w + d, nw), z), device_id_type=MESH
        )
        return carry

    lax.fori_loop(1, nw, greet, 0)
    for neighbour in (left, right):
        pl.semaphore_signal(barrier, inc=1, device_id=(w, neighbour), device_id_type=MESH)
    pl.semaphore_wait(barrier, nw + 1)

    pairs = ((main_ref, omain), (side_ref, oside))

    def first(d, part):
        source, target = pairs[part]
        peer = lax.rem(w + d, nw)
        return pltpu.make_async_remote_copy(
            src_ref=source.at[peer],
            dst_ref=target.at[z, w],
            send_sem=s1.at[part, d],
            recv_sem=r1.at[part, d],
            device_id=(peer, z),
            device_id_type=MESH,
        )

    def send(d, carry):
        for part in range(2):
            first(d, part).start()
        return carry

    for part in range(2):
        source, target = pairs[part]
        pltpu.make_async_copy(source.at[w], target.at[z, w], r1.at[part, 0]).start()
    lax.fori_loop(1, nw, send, 0)

    def arrived(c):
        def one(i, carry):
            origin = c * size + i
            d = lax.rem(w - origin + nw, nw)
            for part in range(2):
                source, target = pairs[part]
                pltpu.make_async_copy(
                    source.at[origin], target.at[z, origin], r1.at[part, d]
                ).wait()
            return carry

        lax.fori_loop(0, size, one, 0)

    def step(way, hop, c, part):
        plane = lax.rem(z - (hop - 1) + nz, nz) if way == 0 else lax.rem(z + (hop - 1), nz)
        block = pairs[part][1].at[plane, pl.ds(c * size, size)]
        return pltpu.make_async_remote_copy(
            src_ref=block,
            dst_ref=block,
            send_sem=s2.at[way, hop - 1, c, part],
            recv_sem=r2.at[way, hop - 1, c, part],
            device_id=(w, right if way == 0 else left),
            device_id_type=MESH,
        )

    def travels(way, hop, c):
        return hop < hops or (c < CHUNKS // 2) == (way == 0)

    for hop in range(hops + 1):
        for c in range(CHUNKS):
            if hop == 0:
                arrived(c)
            for way in range(2):
                if hop > 0 and travels(way, hop, c):
                    for part in range(2):
                        step(way, hop, c, part).wait_recv()
                if hop < hops and travels(way, hop + 1, c):
                    for part in range(2):
                        step(way, hop + 1, c, part).start()

    def drain(d, carry):
        for part in range(2):
            first(d, part).wait_send()
        return carry

    lax.fori_loop(1, nw, drain, 0)
    for hop in range(1, hops + 1):
        for c in range(CHUNKS):
            for way in range(2):
                if travels(way, hop, c):
                    for part in range(2):
                        step(way, hop, c, part).wait_send()


def dispatch(main, side):
    nw, nz = lax.axis_size("wide"), lax.axis_size("narrow")
    anywhere = pl.BlockSpec(memory_space=pl.ANY)
    return pl.pallas_call(
        functools.partial(dispatch_kernel, nw, nz),
        out_shape=(
            jax.ShapeDtypeStruct((nz,) + main.shape, main.dtype),
            jax.ShapeDtypeStruct((nz,) + side.shape, side.dtype),
        ),
        in_specs=[anywhere, anywhere],
        out_specs=(anywhere, anywhere),
        scratch_shapes=[
            pltpu.SemaphoreType.DMA((2, nw)),
            pltpu.SemaphoreType.DMA((2, nw)),
            pltpu.SemaphoreType.DMA((2, nz // 2, CHUNKS, 2)),
            pltpu.SemaphoreType.DMA((2, nz // 2, CHUNKS, 2)),
        ],
        compiler_params=pltpu.CompilerParams(collective_id=0, has_side_effects=True),
        name="dispatch_rows",
    )(main, side)


def unpack_side(side):
    r, c = iota((8 * NE, 8 * NE), 0), iota((8 * NE, 8 * NE), 1)
    ordered = mm(onehot(c == (r % NE) * 8 + r // NE), side.astype(BF16))
    extra = jnp.concatenate(
        [ordered[k * NE : (k + 1) * NE] for k in range(D // 128)], axis=1
    ).astype(BF16)
    repeat = onehot(iota((128, NE * MAIN), 0) == iota((128, NE * MAIN), 1) % MAIN)
    own = iota((NE, NE * MAIN), 1) // MAIN == iota((NE, NE * MAIN), 0)
    diagonal = iota((NE, NE), 0) == iota((NE, NE), 1)
    gates, gates_extra = [], []
    for k in (6, 7):
        g = ordered[k * NE : (k + 1) * NE]
        gates.append(jnp.where(own, mm(g.astype(BF16), repeat), 0.0))
        gates_extra.append(jnp.where(diagonal, g[:, MAIN : MAIN + 1], 0.0))
    return (
        extra,
        jnp.concatenate(gates, axis=0).astype(BF16),
        jnp.concatenate(gates_extra, axis=0).astype(BF16),
    )


def gelu_and_slope(x):
    a, b = 0.7978845608028654, 0.044715
    square = x * x
    t = jnp.tanh(a * x * (1.0 + b * square))
    half = 0.5 * (1.0 + t)
    slope = half + 0.5 * x * (1.0 - t * t) * (a * (1.0 + 3.0 * b * square))
    return (x * half).astype(BF16), slope.astype(BF16)


def sequence_order(transposed):
    n = 16 * NE
    a, b = (1, 0) if transposed else (0, 1)
    r, c = iota((n, n), a), iota((n, n), b)
    return onehot(c == (r % 8) * (2 * NE) + ((r // 8) % 2) * NE + r // 16)


def expert_kernel(main_ref, side_ref, up_ref, down_ref, slope_ref, slope_x_ref, acts_ref, part_ref, acts):
    plane = pl.program_id(0)
    extra, gates, gates_extra = unpack_side(side_ref[0])
    act, slope = gelu_and_slope(mm(main_ref[0], up_ref[...]))
    act_x, slope_x = gelu_and_slope(mm(extra, up_ref[...]))
    slope_ref[0] = slope
    slope_x_ref[0] = slope_x
    acts[plane] = (mm(gates, act) + mm(gates_extra, act_x)).astype(BF16)

    @pl.when(plane == pl.num_programs(0) - 1)
    def _():
        ordered = mm(sequence_order(False), acts[...].reshape(16 * NE, FB)).astype(BF16)
        acts_ref[...] = ordered
        part_ref[...] = mm(ordered, down_ref[...]).astype(BF16)


def experts(main, side, up, down):
    nz = main.shape[0]
    whole = lambda shape: pl.BlockSpec(shape, lambda p: (0,) * len(shape))
    each = lambda shape: pl.BlockSpec((1,) + shape, lambda p: (p,) + (0,) * len(shape))
    return pl.pallas_call(
        expert_kernel,
        grid=(nz,),
        in_specs=[each((NE * MAIN, D)), each((8 * NE, 128)), whole((D, FB)), whole((FB, D))],
        out_specs=(
            each((NE * MAIN, FB)),
            each((NE, FB)),
            whole((16 * NE, FB)),
            whole((16 * NE, D)),
        ),
        out_shape=(
            jax.ShapeDtypeStruct((nz, NE * MAIN, FB), BF16),
            jax.ShapeDtypeStruct((nz, NE, FB), BF16),
            jax.ShapeDtypeStruct((16 * NE, FB), BF16),
            jax.ShapeDtypeStruct((16 * NE, D), BF16),
        ),
        scratch_shapes=[pltpu.VMEM((nz, 2 * NE, FB), BF16)],
        compiler_params=pltpu.CompilerParams(vmem_limit_bytes=VMEM_BYTES),
        name="expert_forward",
    )(main, side, up, down)


def pool_kernel(nw, nz, part_ref, mean_ref, out_ref, got, zsend, zgot, s1, r1, s2, r2, s3, r3):
    w, z = lax.axis_index("wide"), lax.axis_index("narrow")
    rows = part_ref.shape[1]
    barrier = pltpu.get_barrier_semaphore()

    def greet(d, carry):
        pl.semaphore_signal(
            barrier, inc=1, device_id=(lax.rem(w + d, nw), z), device_id_type=MESH
        )
        return carry

    def greet_z(d, carry):
        pl.semaphore_signal(
            barrier, inc=1, device_id=(w, lax.rem(z + d, nz)), device_id_type=MESH
        )
        return carry

    lax.fori_loop(1, nw, greet, 0)
    lax.fori_loop(1, nz, greet_z, 0)
    pl.semaphore_wait(barrier, nw + nz - 2)

    def to_wide(source, target, sends, recvs, d):
        return pltpu.make_async_remote_copy(
            src_ref=source,
            dst_ref=target,
            send_sem=sends.at[d],
            recv_sem=recvs.at[d],
            device_id=(lax.rem(w + d, nw), z),
            device_id_type=MESH,
        )

    def scatter(d):
        return to_wide(part_ref.at[lax.rem(w + d, nw)], got.at[d], s1, r1, d)

    def across(d):
        return pltpu.make_async_remote_copy(
            src_ref=zsend,
            dst_ref=zgot.at[d],
            send_sem=s2.at[d],
            recv_sem=r2.at[d],
            device_id=(w, lax.rem(z + d, nz)),
            device_id_type=MESH,
        )

    def gather(d):
        return to_wide(out_ref.at[w], out_ref.at[w], s3, r3, d)

    def gathered(d):
        block = out_ref.at[lax.rem(w - d + nw, nw)]
        return to_wide(block, block, s3, r3, d)

    def each(count, act):
        def one(d, carry):
            act(d)
            return carry

        lax.fori_loop(1, count, one, 0)

    def summed(count, copy, buffer, start):
        def one(d, total):
            copy(d).wait_recv()
            return total + buffer[d].astype(F32)

        return lax.fori_loop(1, count, one, start)

    each(nw, lambda d: scatter(d).start())
    total = summed(nw, scatter, got, part_ref[w].astype(F32)) * (1.0 / SEQ)
    row = iota((rows, 1), 0)
    total = total + jnp.where(row == z, mean_ref[0:1], 0.0)
    total = total + jnp.where(row == z + rows // 2, mean_ref[1:2], 0.0)
    zsend[...] = total.astype(BF16)
    each(nz, lambda d: across(d).start())
    total = summed(nz, across, zgot, total)
    out_ref[w] = total.astype(out_ref.dtype)
    each(nw, lambda d: gather(d).start())
    each(nw, lambda d: gathered(d).wait_recv())
    each(nw, lambda d: scatter(d).wait_send())
    each(nz, lambda d: across(d).wait_send())
    each(nw, lambda d: gather(d).wait_send())


def pool(part, mean):
    nw, nz = lax.axis_size("wide"), lax.axis_size("narrow")
    rows = part.shape[1]
    wide_sems = [pltpu.SemaphoreType.DMA((nw,))] * 2
    vmem = pl.BlockSpec(memory_space=pltpu.VMEM)
    return pl.pallas_call(
        functools.partial(pool_kernel, nw, nz),
        out_shape=jax.ShapeDtypeStruct((nw, rows, part.shape[2]), F32),
        in_specs=[vmem, vmem],
        out_specs=vmem,
        scratch_shapes=[
            pltpu.VMEM(part.shape, BF16),
            pltpu.VMEM(part.shape[1:], BF16),
            pltpu.VMEM((nz,) + part.shape[1:], BF16),
            *wide_sems,
            pltpu.SemaphoreType.DMA((nz,)),
            pltpu.SemaphoreType.DMA((nz,)),
            *wide_sems,
        ],
        compiler_params=pltpu.CompilerParams(
            collective_id=1, has_side_effects=True, vmem_limit_bytes=VMEM_BYTES
        ),
        name="pooled_rows",
    )(part, mean)


def row_gradients(pooled, positive):
    pairs = 8 * NE
    query = pooled[:, :8].reshape(pairs, D)
    document = pooled[:, 8:].reshape(pairs, D)
    length_q = jnp.sqrt(jnp.sum(query * query, axis=-1, keepdims=True) + EPS)
    length_d = jnp.sqrt(jnp.sum(document * document, axis=-1, keepdims=True) + EPS)
    unit_q, unit_d = query / length_q, document / length_d
    weights = jnp.exp(mm(unit_q, unit_d, 1, 1, HIGHEST) * WARMTH)
    probs = weights / jnp.sum(weights, axis=1, keepdims=True)
    target = jnp.where(positive == iota((pairs, pairs), 1), 1.0, 0.0)
    excess = (probs - target) * (LOSS_SCALE * WARMTH)
    grad_q = mm(excess, unit_d, 1, 0, HIGHEST)
    grad_d = mm(excess, unit_q, 0, 0, HIGHEST)

    def back(unit, grad, length):
        inner = jnp.sum(unit * grad, axis=-1, keepdims=True)
        return ((grad - unit * inner) / (length * float(SEQ))).reshape(NE, 8, D)

    both = [back(unit_q, grad_q, length_q), back(unit_d, grad_d, length_d)]
    return jnp.concatenate(both, axis=1).reshape(16 * NE, D).astype(BF16)


def gradient_kernel(
    pooled_ref, positive_ref, acts_ref, down_ref, main_ref, side_ref, slope_ref, slope_x_ref,
    grad_up_ref, grad_down_ref, spread,
):
    plane = pl.program_id(0)

    @pl.when(plane == 0)
    def _():
        dy = row_gradients(pooled_ref[...], positive_ref[...])
        grad_down_ref[...] = mm(acts_ref[...], dy, 0, 0)
        back = mm(dy, down_ref[...], 1, 1).astype(BF16)
        spread[...] = (
            mm(sequence_order(True), back).astype(BF16).reshape(spread.shape)
        )
        grad_up_ref[...] = jnp.zeros_like(grad_up_ref)

    extra, gates, gates_extra = unpack_side(side_ref[0])
    back = spread[plane]
    dpre = (mm(gates, back, 0, 0) * slope_ref[0].astype(F32)).astype(BF16)
    dpre_x = (mm(gates_extra, back, 0, 0) * slope_x_ref[0].astype(F32)).astype(BF16)
    grad_up_ref[...] += mm(main_ref[0], dpre, 0, 0) + mm(extra, dpre_x, 0, 0)


def gradients(pooled, positive, acts, down, main, side, slope, slope_x):
    nz = main.shape[0]
    whole = lambda shape: pl.BlockSpec(shape, lambda p: (0,) * len(shape))
    each = lambda shape: pl.BlockSpec((1,) + shape, lambda p: (p,) + (0,) * len(shape))
    return pl.pallas_call(
        gradient_kernel,
        grid=(nz,),
        in_specs=[
            whole(pooled.shape),
            whole(positive.shape),
            whole(acts.shape),
            whole((FB, D)),
            each((NE * MAIN, D)),
            each((8 * NE, 128)),
            each((NE * MAIN, FB)),
            each((NE, FB)),
        ],
        out_specs=(whole((D, FB)), whole((FB, D))),
        out_shape=(
            jax.ShapeDtypeStruct((D, FB), F32),
            jax.ShapeDtypeStruct((FB, D), F32),
        ),
        scratch_shapes=[pltpu.VMEM((nz, 2 * NE, FB), BF16)],
        compiler_params=pltpu.CompilerParams(vmem_limit_bytes=VMEM_BYTES),
        name="expert_gradients",
    )(pooled, positive, acts, down, main, side, slope, slope_x)


def body(pair_tokens, expert_ids, positive, w_qkv, w_out, w_router, w_up, w_down):
    nz = lax.axis_size("narrow")
    main, side, mean = front(
        pair_tokens.reshape(TOK, D), expert_ids.reshape(TOK, 2), w_qkv, w_out, w_router
    )
    main, side = dispatch(main.reshape(NE, MAIN, D), side.reshape(NE, 8, 128))
    main = main.reshape(nz, NE * MAIN, D)
    side = side.reshape(nz, NE * 8, 128)
    slope, slope_x, acts, part = experts(main, side, w_up[0], w_down[0])
    pooled = pool(part.reshape(NE, 16, D), mean)
    grad_up, grad_down = gradients(
        pooled, positive.reshape(-1, 1), acts, w_down[0], main, side, slope, slope_x
    )
    return (grad_up[None], grad_down[None])


def solution(mesh):
    return jax.shard_map(
        body,
        mesh=mesh,
        in_specs=(
            P(("wide", "narrow"), None, None, None),
            P(("wide", "narrow"), None, None),
            P(),
            P(),
            P(),
            P(),
            P("wide", None, "narrow"),
            P("wide", "narrow", None),
        ),
        out_specs=(P("wide", None, "narrow"), P("wide", "narrow", None)),
        check_vma=False,
    )
```

time: 791 us -> 198 us (0.25)
  the two profiles are of different devices: /device:TPU:1 before, /device:TPU:89 now
where the time goes in v1:
time: 198 us
  Pallas kernels  192 us (97%)
  local copies, waits for them, and re-layouts  4.54 us (2%)
    pallas_call x1, Pallas kernels, dispatch(): pl.pallas_call(functools.partial(dispatch_kernel, nw, nz), out_shape=(jax...  89.3 us
    pallas_call x1, Pallas kernels, pool(): pl.pallas_call(functools.partial(pool_kernel, nw, nz), out_shape=jax.Shap...  60.5 us
    pallas_call x1, Pallas kernels, gradients(): pl.pallas_call(gradient_kernel, grid=(nz,), in_specs=[whole(pooled.shape)...  19.1 us
    pallas_call x1, Pallas kernels, experts(): pl.pallas_call(expert_kernel, grid=(nz,), in_specs=[each((NE * MAIN, D)),...  13.8 us
    pallas_call x1, Pallas kernels, front(): pl.pallas_call(front_kernel, out_shape=(jax.ShapeDtypeStruct((NE * MAIN,...  9.79 us

profile of v1, /device:TPU:89, one launch (start us, length us, event | category | flops | bytes accessed | tf_op | source)
XLA Modules:
  0.0 197.6 jit_solution(1553944226548979048)
XLA Ops:
  0.6 1.5 copy.12
  2.1 1.5 copy.14.positive_ref
  3.6 1.6 copy.13.wr_ref
  5.2 9.8 %attention_and_slots.1 = (bf16[512,768]{1,0:T(8,128)(2,1)}, f32[256,128]{1,0:T(8,128)}, f32[8,768]{1,0:T(8,128)}) custom-call(bf16[256,768]{1,0:T(8,128)(2,1)} %bitcast.22, s32[256,2]{1,0:T(8,128)} %bitcast.21, bf16[768,2304]{1,0:T(8,128)(2,1)} %wqkv_ref.1, bf16[768,768]{1,0:T(8,128)(2,1)} %wout_ref.1, bf16[768,32]{1,0:T(8,128)(2,1)} %copy.13.wr_ref), custom_call_target="tpu_custom_call" | custom-call | tf_op jit(solution)/shard_map/attention_and_slots/pallas_call | solution.py:116
  15.0 89.3 %dispatch_rows.1 = (bf16[8,32,16,768]{3,2,1,0:T(8,128)(2,1)}, f32[8,32,8,128]{3,2,1,0:T(8,128)}) custom-call(bf16[32,16,768]{2,1,0:T(8,128)(2,1)} %bitcast.18, f32[32,8,128]{2,1,0:T(8,128)} %bitcast.23), custom_call_target="tpu_custom_call" | custom-call | tf_op jit(solution)/shard_map/dispatch_rows/pallas_call | solution.py:228
  104.3 13.8 %expert_forward.1 = (bf16[8,512,384]{2,1,0:T(8,128)(2,1)}, bf16[8,32,384]{2,1,0:T(8,128)(2,1)}, bf16[512,384]{1,0:T(8,128)(2,1)}, bf16[512,768]{1,0:T(8,128)(2,1)}) custom-call(bf16[8,512,768]{2,1,0:T(8,128)(2,1)} %bitcast.12, f32[8,256,128]{2,1,0:T(8,128)} %bitcast.14, bf16[768,384]{1,0:T(8,128)(2,1)} %bitcast.20, bf16[384,768]{1,0:T(8,128)(2,1)} %bitcast.16), custom_call_target="tpu_custom_call" | custom-call | tf_op jit(solution)/shard_map/expert_forward/pallas_call | solution.py:304
  118.1 60.5 %pooled_rows.1.pooled_ref = f32[32,16,768]{2,1,0:T(8,128)} custom-call(bf16[32,16,768]{2,1,0:T(8,128)(2,1)} %bitcast.19, f32[8,768]{1,0:T(8,128)} %get-tuple-element.18.mean_ref), custom_call_target="tpu_custom_call" | custom-call | tf_op jit(solution)/shard_map/pooled_rows/pallas_call | solution.py:412
  178.6 19.1 %expert_gradients.1 = (f32[768,384]{1,0:T(8,128)}, f32[384,768]{1,0:T(8,128)}) custom-call(f32[32,16,768]{2,1,0:T(8,128)} %pooled_rows.1.pooled_ref, s32[256,1]{1,0:T(8,128)} %copy.14.positive_ref, bf16[512,384]{1,0:T(8,128)(2,1)} %get-tuple-element.19.acts_ref, bf16[384,768]{1,0:T(8,128)(2,1)} %bitcast.17, bf16[8,512,768]{2,1,0:T(8,128)(2,1)} %bitcast.13, ...), custom_call_target="tpu_custom_call" | custom-call | tf_op jit(solution)/shard_map/expert_gradients/pallas_call | solution.py:482

commit v2 on v0

v2 whole, which is shorter than its diff:
```python
import functools

import jax
import jax.numpy as jnp
from jax import lax
from jax.experimental import pallas as pl
from jax.experimental.pallas import tpu as pltpu
from jax.sharding import PartitionSpec as P

D = 768
FB = 384
SEQ = 128
TOK = 256
NE = 32
MAIN = 16
ROW = D + 128
CHUNKS = 4
SIZE = NE // CHUNKS
CROWS = SIZE * MAIN
EPS = 1e-06
WARMTH = 20.0
LOSS_SCALE = 64.0
VMEM_BYTES = 56 * 2**20
MESH = pl.DeviceIdType.MESH
HIGHEST = lax.Precision.HIGHEST
F32, BF16, I32 = jnp.float32, jnp.bfloat16, jnp.int32


def mm(a, b, ca=1, cb=0, precision=None):
    return lax.dot_general(
        a, b, (((ca,), (cb,)), ((), ())), precision=precision, preferred_element_type=F32
    )


def iota(shape, axis):
    return lax.broadcasted_iota(I32, shape, axis)


def onehot(condition):
    return jnp.where(condition, 1.0, 0.0).astype(BF16)


def rms(v):
    return v * lax.rsqrt(jnp.mean(v * v, axis=-1, keepdims=True) + EPS)


def front(x_ref, ids_ref, wqkv_ref, wout_ref, wr_ref, blocks, mixed):
    normed = rms(x_ref[...].astype(F32)).astype(BF16)
    wide = 256
    same_head = onehot(iota((wide, wide), 0) // 64 == iota((wide, wide), 1) // 64)
    low = iota((SEQ, 128), 1) < 64
    ones = jnp.ones((SEQ, 128), BF16)

    def head_rms(v):
        square = v * v
        high = square.astype(BF16)
        rest = (square - high.astype(F32)).astype(BF16)
        mean = (mm(high, same_head) + mm(rest, same_head)) * (1.0 / 64.0)
        return (v * lax.rsqrt(mean + EPS)).astype(BF16)

    for block in range(D // wide):
        at = block * wide
        q = head_rms(mm(normed, wqkv_ref[:, at : at + wide]))
        k = head_rms(mm(normed, wqkv_ref[:, D + at : D + at + wide]))
        v = mm(normed, wqkv_ref[:, 2 * D + at : 2 * D + at + wide]).astype(BF16)
        for s in range(TOK // SEQ):
            rows = slice(s * SEQ, (s + 1) * SEQ)
            for c in range(wide // 128):
                lanes = slice(c * 128, (c + 1) * 128)
                qc, kc = q[rows, lanes], k[rows, lanes]
                values = jnp.concatenate([v[rows, lanes], ones], axis=1)
                heads = []
                for half in range(2):
                    qh = jnp.where(low if half == 0 else ~low, qc, jnp.zeros_like(qc))
                    weights = jnp.exp(mm(qh, kc, 1, 1) * 0.125).astype(BF16)
                    both = mm(weights, values)
                    heads.append(both[:, :128] / both[:, 128:])
                mixed[rows, at + c * 128 : at + (c + 1) * 128] = jnp.where(
                    low, heads[0], heads[1]
                ).astype(BF16)

    h = (x_ref[...].astype(F32) + mm(mixed[...], wout_ref[...])).astype(BF16).astype(F32)
    mean_q = jnp.mean(h[:SEQ], axis=0, keepdims=True)
    mean_d = jnp.mean(h[SEQ:], axis=0, keepdims=True)
    z = rms(h).astype(BF16)

    logits = mm(wr_ref[...], z, 1, 1)
    names = iota((NE, TOK), 0)
    here = (ids_ref[0:1, :] == names) | (ids_ref[1:2, :] == names)
    earlier = onehot(iota((TOK, TOK), 0) < iota((TOK, TOK), 1))
    rank = jnp.where(here, mm(onehot(here), earlier), -1.0)
    both_logits = jnp.sum(jnp.where(here, logits, 0.0), axis=0, keepdims=True)
    gate = jnp.where(here, 1.0 / (1.0 + jnp.exp(both_logits - 2.0 * logits)), 0.0)

    spread = onehot(iota((NE * MAIN, NE), 0) // MAIN == iota((NE * MAIN, NE), 1))
    slot = (iota((NE * MAIN, TOK), 0) % MAIN).astype(F32)
    main = mm(onehot(mm(spread, rank.astype(BF16)) == slot), z).astype(BF16)
    blocks[:, :, :D] = main.reshape(NE, MAIN, D)

    extra = mm(onehot(rank == float(MAIN)), z).astype(BF16)
    lane = iota((NE, 128), 1)
    gates_q = jnp.zeros((NE, 128), F32)
    gates_d = jnp.zeros((NE, 128), F32)
    for s in range(MAIN + 1):
        chosen = jnp.where(rank == float(s), gate, 0.0)
        gates_q = jnp.where(lane == s, jnp.sum(chosen[:, :SEQ], axis=1, keepdims=True), gates_q)
        gates_d = jnp.where(lane == s, jnp.sum(chosen[:, SEQ:], axis=1, keepdims=True), gates_d)
    parts = [extra[:, c * 128 : (c + 1) * 128] for c in range(D // 128)]
    stacked = jnp.concatenate(parts + [gates_q.astype(BF16), gates_d.astype(BF16)], axis=0)
    r, c = iota((NE * MAIN, 8 * NE), 0), iota((NE * MAIN, 8 * NE), 1)
    side = mm(onehot(c == (r % MAIN) * NE + r // MAIN), stacked).astype(BF16)
    blocks[:, :, D:] = side.reshape(NE, MAIN, 128)
    return mean_q, mean_d


def gelu_and_slope(x):
    a, b = 0.7978845608028654, 0.044715
    square = x * x
    t = jnp.tanh(a * x * (1.0 + b * square))
    half = 0.5 * (1.0 + t)
    slope = half + 0.5 * x * (1.0 - t * t) * (a * (1.0 + 3.0 * b * square))
    return (x * half).astype(BF16), slope.astype(BF16)


def expert_chunk(plane, c, rows, up_ref, turned, extras, slopes, gates, acts):
    q = plane * CHUNKS + c
    block = rows[plane, pl.ds(c * SIZE, SIZE)].reshape(CROWS, ROW)
    main = block[:, :D]
    turned[q] = main.T
    r, col = iota((128, CROWS), 0), iota((128, CROWS), 1)
    take = onehot((col == (r % MAIN) * MAIN + r // MAIN) & (r % MAIN < SIZE))
    side = mm(take, block[:, D:])
    extra = jnp.concatenate(
        [side[k * MAIN : (k + 1) * MAIN] for k in range(D // 128)], axis=1
    ).astype(BF16)
    extras[q] = extra
    own = jnp.concatenate([side[6 * MAIN : 6 * MAIN + SIZE], side[7 * MAIN : 7 * MAIN + SIZE]])
    wide = CROWS + 128
    s, j = iota((128, wide), 0), iota((128, wide), 1)
    repeat = onehot(s == jnp.where(j < CROWS, j % MAIN, MAIN))
    i, j = iota((2 * SIZE, wide), 0), iota((2 * SIZE, wide), 1)
    mine = jnp.where(j < CROWS, j // MAIN, j - CROWS) == i % SIZE
    gate = jnp.where(mine, mm(own.astype(BF16), repeat), 0.0).astype(BF16)
    gates[q] = gate
    act, slope = gelu_and_slope(mm(main, up_ref[...]))
    act_x, slope_x = gelu_and_slope(mm(extra, up_ref[...]))
    slopes[q, :CROWS] = slope
    slopes[q, CROWS:] = slope_x
    total = mm(gate[:, :CROWS], act) + mm(gate[:, CROWS : CROWS + MAIN], act_x)
    acts[q] = total.astype(BF16)


def wide_of(i):
    return (i % (NE // 2)) * 2 + i // (NE // 2)


def sequence_order(transposed):
    n = 16 * NE
    a, b = (1, 0) if transposed else (0, 1)
    r, c = iota((n, n), a), iota((n, n), b)
    w = wide_of(r // 16)
    row = ((r % 8) * CHUNKS + w // SIZE) * 16 + ((r // 8) % 2) * 8 + w % SIZE
    return onehot(c == row)


def split(v):
    high = v.astype(BF16)
    return high, (v - high.astype(F32)).astype(BF16)


def row_gradients(pooled, positive):
    pairs = 8 * NE
    query = pooled[:, :8].reshape(pairs, D)
    document = pooled[:, 8:].reshape(pairs, D)
    query_b, document_b = query.astype(BF16), document.astype(BF16)
    inverse_q = lax.rsqrt(jnp.sum(query * query, axis=-1, keepdims=True) + EPS)
    inverse_d = lax.rsqrt(jnp.sum(document * document, axis=-1, keepdims=True) + EPS)
    squares = mm(jnp.ones((8, D), F32), document * document, 1, 1, HIGHEST)
    inverse_row = lax.rsqrt(squares[0:1] + EPS)
    weights = jnp.exp(mm(query_b, document_b, 1, 1) * (inverse_q * WARMTH) * inverse_row)
    probs = weights / jnp.sum(weights, axis=1, keepdims=True)

    def number(j):
        return wide_of(j // 8) * 8 + j % 8

    r, c = iota((pairs, pairs), 0), iota((pairs, pairs), 1)
    target = mm(onehot(number(r) == c), onehot(number(r) == positive), 1, 1)
    excess = (probs - target) * (LOSS_SCALE * WARMTH)
    high, rest = split(excess * inverse_row)
    grad_q = mm(high, document_b) + mm(rest, document_b)
    high, rest = split(excess * inverse_q)
    grad_d = mm(high, query_b, 0, 0) + mm(rest, query_b, 0, 0)

    def back(row, grad, inverse):
        unit = row * inverse
        inner = jnp.sum(unit * grad, axis=-1, keepdims=True)
        return ((grad - unit * inner) * (inverse * (1.0 / SEQ))).reshape(NE, 8, D)

    both = [back(query, grad_q, inverse_q), back(document, grad_d, inverse_d)]
    return jnp.concatenate(both, axis=1).reshape(16 * NE, D).astype(BF16)


def each(start, stop, act):
    def one(i, carry):
        act(i)
        return carry

    lax.fori_loop(start, stop, one, 0)


def step_kernel(
    nw, nz,
    x_ref, ids_ref, positive_ref, wqkv_ref, wout_ref, wr_ref, up_ref, down_ref,
    grad_up_ref, grad_down_ref,
    blocks, mixed, rows, turned, extras, slopes, gates, acts, spread, dpre, dpre_x,
    ordered, part, lent, half, got, zsend, zgot, pooled,
    s1, r1, s2, r2, sem_core, s3, r3, s4, r4, s5, r5, s6, r6,
):
    w, z = lax.axis_index("wide"), lax.axis_index("narrow")
    right, left = lax.rem(z + 1, nz), lax.rem(z + nz - 1, nz)
    hops, chips = nz // 2, nw // 2
    chip, core = w // 2, lax.rem(w, 2)
    sibling = w + 1 - 2 * core

    barrier = pltpu.get_barrier_semaphore()

    def greet(peer):
        pl.semaphore_signal(barrier, inc=1, device_id=peer, device_id_type=MESH)

    each(1, nw, lambda d: greet((lax.rem(w + d, nw), z)))
    each(1, nz, lambda d: greet((w, lax.rem(z + d, nz))))

    mean_q, mean_d = front(x_ref, ids_ref, wqkv_ref, wout_ref, wr_ref, blocks, mixed)

    pl.semaphore_wait(barrier, nw + nz - 2)

    def copy(source, target, send, receive, peer):
        return pltpu.make_async_remote_copy(
            src_ref=source, dst_ref=target, send_sem=send, recv_sem=receive,
            device_id=peer, device_id_type=MESH,
        )

    def first(d):
        peer = lax.rem(w + d, nw)
        return copy(blocks.at[peer], rows.at[z, w], s1.at[d], r1.at[d], (peer, z))

    pltpu.make_async_copy(blocks.at[w], rows.at[z, w], r1.at[0]).start()
    each(1, nw, lambda d: first(d).start())

    def arrived(c):
        def one(i):
            origin = c * SIZE + i
            pltpu.make_async_copy(
                blocks.at[origin], rows.at[z, origin], r1.at[lax.rem(w - origin + nw, nw)]
            ).wait()

        each(0, SIZE, one)

    def plane_at(way, hop):
        return lax.rem(z + nz - hop, nz) if way == 0 else lax.rem(z + hop, nz)

    def move(way, hop, c):
        block = rows.at[plane_at(way, hop - 1), pl.ds(c * SIZE, SIZE)]
        return copy(
            block, block, s2.at[way, hop - 1, c], r2.at[way, hop - 1, c],
            (w, right if way == 0 else left),
        )

    def work(plane, c):
        expert_chunk(plane, c, rows, up_ref, turned, extras, slopes, gates, acts)

    def home(c):
        arrived(c)
        for way in range(2):
            move(way, 1, c).start()
        work(z, c)

    each(0, CHUNKS, home)

    def both_ways(hop, c, onward):
        for way in range(2):
            move(way, hop, c).wait_recv()
            if way in onward:
                move(way, hop + 1, c).start()
        each(0, 2, lambda way: work(lax.rem(z + nz + (2 * way - 1) * hop, nz), c))

    each(0, (hops - 2) * CHUNKS, lambda i: both_ways(1 + i // CHUNKS, lax.rem(i, CHUNKS), (0, 1)))
    each(0, CHUNKS // 2, lambda c: both_ways(hops - 1, c, (0,)))
    each(CHUNKS // 2, CHUNKS, lambda c: both_ways(hops - 1, c, (1,)))

    def last(i):
        for way in range(2):
            move(way, hops, i + way * (CHUNKS // 2)).wait_recv()
        each(0, 2, lambda way: work(lax.rem(z + hops, nz), i + way * (CHUNKS // 2)))

    each(0, CHUNKS // 2, last)

    side = NE // 2 * 16
    ordered[...] = mm(sequence_order(False), acts[...].reshape(16 * NE, FB)).astype(BF16)

    def partial(which):
        return mm(ordered[pl.ds(pl.multiple_of(which * side, side), side)], down_ref[...])

    lent[...] = partial(1 - core).astype(BF16).reshape(lent.shape)
    swap = copy(lent, half, sem_core.at[0], sem_core.at[1], (sibling, z))
    swap.start()
    part[...] = partial(core).reshape(part.shape)
    swap.wait_recv()
    part[...] = part[...] + half[...].astype(F32)
    swap.wait_send()
    lent[...] = part[...].astype(BF16)

    def peer_chip(d):
        return lax.rem(chip + d, chips)

    def scatter(d):
        return copy(
            lent.at[peer_chip(d)], got.at[d], s3.at[d], r3.at[d], (peer_chip(d) * 2 + core, z)
        )

    def across(d):
        return copy(zsend, zgot.at[d], s4.at[d], r4.at[d], (w, lax.rem(z + d, nz)))

    def gather(d, origin):
        block = pooled.at[core, origin]
        return copy(block, block, s5.at[d], r5.at[d], (peer_chip(d) * 2 + core, z))

    def lend(d, origin, holder):
        block = pooled.at[holder, origin]
        return copy(block, block, s6.at[d], r6.at[d], (sibling, z))

    def summed(count, one_copy, buffer, start):
        def one(d, total):
            one_copy(d).wait_recv()
            return total + buffer[d].astype(F32)

        return lax.fori_loop(1, count, one, start)

    each(1, chips, lambda d: scatter(d).start())
    total = summed(chips, scatter, got, part[chip]) * (1.0 / SEQ)
    row = iota((16, 1), 0)
    total = total + jnp.where(row == z, mean_q, 0.0) + jnp.where(row == z + 8, mean_d, 0.0)
    zsend[...] = total.astype(BF16)
    each(1, nz, lambda d: across(d).start())
    pooled[core, chip] = summed(nz, across, zgot, total).astype(BF16)
    each(1, chips, lambda d: gather(d, chip).start())
    lend(0, chip, core).start()

    def pass_on(d):
        origin = lax.rem(chip - d + chips, chips)
        gather(d, origin).wait_recv()
        lend(d, origin, core).start()

    each(1, chips, pass_on)
    each(0, chips, lambda d: lend(d, lax.rem(chip - d + chips, chips), 1 - core).wait_recv())

    dy = row_gradients(pooled[...].reshape(NE, 16, D).astype(F32), positive_ref[...])
    grad_down_ref[...] = mm(ordered[...], dy, 0, 0)
    back = mm(dy, down_ref[...], 1, 1).astype(BF16)
    spread[...] = mm(sequence_order(True), back).astype(BF16).reshape(spread.shape)

    def before(q):
        gate, back = gates[q], spread[q]
        slope = slopes[q].astype(F32)
        dpre[q] = (mm(gate[:, :CROWS], back, 0, 0) * slope[:CROWS]).astype(BF16)
        dpre_x[q] = (
            mm(gate[:, CROWS : CROWS + MAIN], back, 0, 0) * slope[CROWS:]
        ).astype(BF16)

    each(0, nz * CHUNKS, before)
    extra_rows = nz * CHUNKS * MAIN
    grad_up_ref[...] = mm(
        extras[...].reshape(extra_rows, D), dpre_x[...].reshape(extra_rows, FB), 0, 0
    )

    def add(p):
        left_side = jnp.concatenate([turned[p * CHUNKS + c] for c in range(CHUNKS)], axis=1)
        right_side = dpre[pl.ds(p * CHUNKS, CHUNKS)].reshape(CHUNKS * CROWS, FB)
        grad_up_ref[...] += mm(left_side, right_side)

    each(0, nz, add)

    each(1, nw, lambda d: first(d).wait_send())
    for way in range(2):
        each(0, (hops - 1) * CHUNKS, lambda i: move(way, 1 + i // CHUNKS, lax.rem(i, CHUNKS)).wait_send())
        each(0, CHUNKS // 2, lambda i: move(way, hops, i + way * (CHUNKS // 2)).wait_send())
    each(1, chips, lambda d: scatter(d).wait_send())
    each(1, nz, lambda d: across(d).wait_send())
    each(1, chips, lambda d: gather(d, chip).wait_send())
    each(0, chips, lambda d: lend(d, lax.rem(chip - d + chips, chips), core).wait_send())


def body(pair_tokens, expert_ids, positive, w_qkv, w_out, w_router, w_up, w_down):
    nw, nz = lax.axis_size("wide"), lax.axis_size("narrow")
    chips, parts = nw // 2, nz * CHUNKS
    dma = pltpu.SemaphoreType.DMA
    vmem = pl.BlockSpec(memory_space=pltpu.VMEM)
    grad_up, grad_down = pl.pallas_call(
        functools.partial(step_kernel, nw, nz),
        out_shape=(
            jax.ShapeDtypeStruct((D, FB), F32),
            jax.ShapeDtypeStruct((FB, D), F32),
        ),
        in_specs=[vmem] * 8,
        out_specs=(vmem, vmem),
        scratch_shapes=[
            pltpu.VMEM((NE, MAIN, ROW), BF16),
            pltpu.VMEM((TOK, D), BF16),
            pltpu.VMEM((nz, nw, MAIN, ROW), BF16),
            pltpu.VMEM((parts, D, CROWS), BF16),
            pltpu.VMEM((parts, MAIN, D), BF16),
            pltpu.VMEM((parts, CROWS + MAIN, FB), BF16),
            pltpu.VMEM((parts, 2 * SIZE, CROWS + 128), BF16),
            pltpu.VMEM((parts, 2 * SIZE, FB), BF16),
            pltpu.VMEM((parts, 2 * SIZE, FB), BF16),
            pltpu.VMEM((parts, CROWS, FB), BF16),
            pltpu.VMEM((parts, MAIN, FB), BF16),
            pltpu.VMEM((16 * NE, FB), BF16),
            pltpu.VMEM((chips, 16, D), F32),
            pltpu.VMEM((chips, 16, D), BF16),
            pltpu.VMEM((chips, 16, D), BF16),
            pltpu.VMEM((chips, 16, D), BF16),
            pltpu.VMEM((16, D), BF16),
            pltpu.VMEM((nz, 16, D), BF16),
            pltpu.VMEM((2, chips, 16, D), BF16),
            dma((nw,)), dma((nw,)),
            dma((2, nz // 2, CHUNKS)), dma((2, nz // 2, CHUNKS)),
            dma((2,)),
            dma((chips,)), dma((chips,)),
            dma((nz,)), dma((nz,)),
            dma((chips,)), dma((chips,)),
            dma((chips,)), dma((chips,)),
        ],
        compiler_params=pltpu.CompilerParams(
            collective_id=0, has_side_effects=True, vmem_limit_bytes=VMEM_BYTES
        ),
        name="contrastive_step",
    )(
        pair_tokens.reshape(TOK, D),
        expert_ids.reshape(TOK, 2).T,
        positive.reshape(1, -1),
        w_qkv,
        w_out,
        w_router.T,
        w_up[0],
        w_down[0],
    )
    return (grad_up[None], grad_down[None])


def solution(mesh):
    return jax.shard_map(
        body,
        mesh=mesh,
        in_specs=(
            P(("wide", "narrow"), None, None, None),
            P(("wide", "narrow"), None, None),
            P(),
            P(),
            P(),
            P(),
            P("wide", None, "narrow"),
            P("wide", "narrow", None),
        ),
        out_specs=(P("wide", None, "narrow"), P("wide", "narrow", None)),
        check_vma=False,
    )
```

time: 791 us -> 151 us (0.19)
  waiting for transfers between devices: 496 us -> 0 us
  Pallas kernels: 0 us -> 147 us
  blocking collectives: 124 us -> 0 us
  local copies, waits for them, and re-layouts: 76.6 us -> 3.47 us
  matrix products: 51.8 us -> 0 us
  between operations: 14.3 us -> 0.65 us
  other arithmetic: 12.8 us -> 0 us
  starting transfers between devices: 8.23 us -> 0 us
    unnamed x5 -> x0, waiting for transfers between devices: 250 us -> none
    all_gather x2 -> x0, waiting for transfers between devices: 151 us -> none  [the longest x1 77 us: body(): lax.all_gather(arrived, 'narrow', axis=0, tiled=True).reshape(-1, width)]
    pallas_call x0 -> x1, Pallas kernels: none -> 147 us  [body(): pl.pallas_call(functools.partial(step_kernel, nw, nz), out_shape=(jax.Sha...]
    reduce_scatter x1 -> x0, waiting for transfers between devices: 77.7 us -> none  [body(): lax.psum_scatter(partial_value.astype(jnp.bfloat16), 'narrow', scatter_di...]
    all_gather x1 -> x0, blocking collectives: 69.7 us -> none  [body(): lax.all_gather(passage_unit_vector, ('wide', 'narrow'), axis=0, tiled=True)]
    all_to_all x2 -> x0, blocking collectives: 54.7 us -> none  [the longest x1 27.4 us: body(): lax.all_to_all(outgoing_grad, 'wide', split_axis=0, concat_axis=0, tiled=...]
    dot_general x11 -> x0, matrix products: 51.8 us -> none  [the longest x2 24.8 us: contract_rows(): lax.dot_general(left, right, (((0,), (0,)), ((), ())), preferred_element_...]
    reshape x7 -> x0, local copies, waits for them, and re-layouts: 27.7 us -> none  [the longest x1 11.3 us: body(): lax.all_gather(arrived, 'narrow', axis=0, tiled=True).reshape(-1, width)]
  transfers between devices with their start and end apart: 5 -> 0, of which waited for: 5 -> 0; matrix products, arithmetic and copies ran while one was open for 0% -> 0% of each run, Pallas kernels for 0% -> 0%
where the time goes in v2:
time: 151 us
  Pallas kernels  147 us (97%)
  local copies, waits for them, and re-layouts  3.47 us (2%)
    pallas_call x1, Pallas kernels, body(): pl.pallas_call(functools.partial(step_kernel, nw, nz), out_shape=(jax.Sha...  147 us
    unnamed x4, local copies, waits for them, and re-layouts  3.47 us

profile of v2, /device:TPU:1, one launch (start us, length us, event | category | flops | bytes accessed | tf_op | source)
XLA Modules:
  0.0 151.0 jit_solution(4295382224533909543)
XLA Ops:
  0.6 146.8 %contrastive_step.1 = (f32[768,384]{1,0:T(8,128)}, f32[384,768]{1,0:T(8,128)}) custom-call(bf16[256,768]{1,0:T(8,128)(2,1)} %bitcast.14, s32[2,256]{1,0:T(2,128)} %bitcast.16, s32[1,256]{1,0:T(1,128)} %bitcast.17, bf16[768,2304]{1,0:T(8,128)(2,1)} %wqkv_ref.1, bf16[768,768]{1,0:T(8,128)(2,1)} %wout_ref.1, bf16[32,768]{1,0:T(8,128)(2,1)} %bitcast.15, ...), custom_call_target="tpu_custom_call" | custom-call | tf_op jit(solution)/shard_map/contrastive_step/pallas_call | solution.py:398
  147.5 0.0 copy-start
  147.5 2.5 %copy.12 = f32[1,768,384]{2,1,0:T(8,128)} copy(f32[1,768,384]{2,1,0:T(8,128)} %bitcast.11) | data formatting | bytes 2359296
  149.9 0.0 copy-done
  149.9 1.0 copy.13
Async XLA Ops:
  147.5 2.5 %copy-start = (f32[384,768]{1,0:T(8,128)S(1)}, f32[384,768]{1,0:T(8,128)}, u32[]{:S(2)}) copy-start(f32[384,768]{1,0:T(8,128)} %get-tuple-element.5) | copy-start | bytes 3538948

commit v3 on v2

--- a/solution.py
+++ b/solution.py
@@ -15,8 +15,11 @@
 MAIN = 16
 ROW = D + 128
 CHUNKS = 4
+AHEAD = 2
 SIZE = NE // CHUNKS
 CROWS = SIZE * MAIN
+SROWS = SIZE * 8
+STRIDE, UNSTRIDE = 11, 3
 EPS = 1e-06
 WARMTH = 20.0
 LOSS_SCALE = 64.0
@@ -44,7 +47,7 @@
     return v * lax.rsqrt(jnp.mean(v * v, axis=-1, keepdims=True) + EPS)
 
 
-def front(x_ref, ids_ref, wqkv_ref, wout_ref, wr_ref, blocks, mixed):
+def front(loads, x_ref, ids_ref, wqkv_ref, wout_ref, wr_ref, blocks, mixed):
     normed = rms(x_ref[...].astype(F32)).astype(BF16)
     wide = 256
     same_head = onehot(iota((wide, wide), 0) // 64 == iota((wide, wide), 1) // 64)
@@ -60,6 +63,7 @@
 
     for block in range(D // wide):
         at = block * wide
+        loads.wait(block)
         q = head_rms(mm(normed, wqkv_ref[:, at : at + wide]))
         k = head_rms(mm(normed, wqkv_ref[:, D + at : D + at + wide]))
         v = mm(normed, wqkv_ref[:, 2 * D + at : 2 * D + at + wide]).astype(BF16)
@@ -79,6 +83,7 @@
                     low, heads[0], heads[1]
                 ).astype(BF16)
 
+    loads.wait(D // wide)
     h = (x_ref[...].astype(F32) + mm(mixed[...], wout_ref[...])).astype(BF16).astype(F32)
     mean_q = jnp.mean(h[:SEQ], axis=0, keepdims=True)
     mean_d = jnp.mean(h[SEQ:], axis=0, keepdims=True)
@@ -122,26 +127,30 @@
     return (x * half).astype(BF16), slope.astype(BF16)
 
 
-def expert_chunk(plane, c, rows, up_ref, turned, extras, slopes, gates, acts):
+def pack_side(block):
+    r, col = iota((SROWS, CROWS), 0), iota((SROWS, CROWS), 1)
+    take = onehot(col == (r % SIZE) * MAIN + r // SIZE)
+    return mm(take, block.reshape(CROWS, 128)).astype(BF16)
+
+
+def expert_chunk(plane, c, rows, sides, up_ref, turned, extras, slopes, gates, acts):
     q = plane * CHUNKS + c
-    block = rows[plane, pl.ds(c * SIZE, SIZE)].reshape(CROWS, ROW)
-    main = block[:, :D]
+    main = rows[plane, pl.ds(c * SIZE, SIZE)].reshape(CROWS, ROW)[:, :D]
     turned[q] = main.T
-    r, col = iota((128, CROWS), 0), iota((128, CROWS), 1)
-    take = onehot((col == (r % MAIN) * MAIN + r // MAIN) & (r % MAIN < SIZE))
-    side = mm(take, block[:, D:])
+    side = sides[q].astype(F32)
     extra = jnp.concatenate(
-        [side[k * MAIN : (k + 1) * MAIN] for k in range(D // 128)], axis=1
-    ).astype(BF16)
+        [side[k * SIZE : (k + 1) * SIZE] for k in range(D // 128)], axis=1
+    )
+    extra = jnp.concatenate([extra, jnp.zeros((MAIN - SIZE, D), F32)]).astype(BF16)
     extras[q] = extra
-    own = jnp.concatenate([side[6 * MAIN : 6 * MAIN + SIZE], side[7 * MAIN : 7 * MAIN + SIZE]])
+    own = side[6 * SIZE :]
     wide = CROWS + 128
     s, j = iota((128, wide), 0), iota((128, wide), 1)
     repeat = onehot(s == jnp.where(j < CROWS, j % MAIN, MAIN))
     i, j = iota((2 * SIZE, wide), 0), iota((2 * SIZE, wide), 1)
     mine = jnp.where(j < CROWS, j // MAIN, j - CROWS) == i % SIZE
     gate = jnp.where(mine, mm(own.astype(BF16), repeat), 0.0).astype(BF16)
-    gates[q] = gate
+    gates[q] = gate[:, : CROWS + MAIN].T
     act, slope = gelu_and_slope(mm(main, up_ref[...]))
     act_x, slope_x = gelu_and_slope(mm(extra, up_ref[...]))
     slopes[q, :CROWS] = slope
@@ -154,12 +163,12 @@
     return (i % (NE // 2)) * 2 + i // (NE // 2)
 
 
-def sequence_order(transposed):
+def sequence_order(w_here, transposed):
     n = 16 * NE
     a, b = (1, 0) if transposed else (0, 1)
     r, c = iota((n, n), a), iota((n, n), b)
-    w = wide_of(r // 16)
-    row = ((r % 8) * CHUNKS + w // SIZE) * 16 + ((r // 8) % 2) * 8 + w % SIZE
+    j = ((w_here + NE - wide_of(r // 16)) * UNSTRIDE) % NE
+    row = ((r % 8) * CHUNKS + j // SIZE) * 16 + ((r // 8) % 2) * 8 + j % SIZE
     return onehot(c == row)
 
 
@@ -210,9 +219,10 @@
 
 def step_kernel(
     nw, nz,
-    x_ref, ids_ref, positive_ref, wqkv_ref, wout_ref, wr_ref, up_ref, down_ref,
+    x_ref, ids_ref, positive_ref, wr_ref, wqkv_hbm, wout_hbm, up_hbm, down_hbm,
     grad_up_ref, grad_down_ref,
-    blocks, mixed, rows, turned, extras, slopes, gates, acts, spread, dpre, dpre_x,
+    wqkv_ref, wout_ref, up_ref, down_ref, load_sems,
+    blocks, mixed, rows, sides, turned, extras, slopes, gates, acts, spread, dpre_x,
     ordered, part, lent, half, got, zsend, zgot, pooled,
     s1, r1, s2, r2, sem_core, s3, r3, s4, r4, s5, r5, s6, r6,
 ):
@@ -222,6 +232,35 @@
     chip, core = w // 2, lax.rem(w, 2)
     sibling = w + 1 - 2 * core
 
+    class loads:
+        steps = [
+            [
+                (
+                    wqkv_hbm.at[:, pl.ds(third * D + block * 256, 256)],
+                    wqkv_ref.at[:, pl.ds(third * D + block * 256, 256)],
+                )
+                for third in range(3)
+            ]
+            for block in range(D // 256)
+        ] + [[(wout_hbm, wout_ref)], [(up_hbm, up_ref)], [(down_hbm, down_ref)]]
+
+        def copies(step):
+            return [
+                pltpu.make_async_copy(source, target, load_sems.at[step, i])
+                for i, (source, target) in enumerate(loads.steps[step])
+            ]
+
+        def start(step):
+            for one in loads.copies(step):
+                one.start()
+
+        def wait(step):
+            for one in loads.copies(step):
+                one.wait()
+
+    for step in range(len(loads.steps)):
+        loads.start(step)
+
     barrier = pltpu.get_barrier_semaphore()
 
     def greet(peer):
@@ -230,7 +269,11 @@
     each(1, nw, lambda d: greet((lax.rem(w + d, nw), z)))
     each(1, nz, lambda d: greet((w, lax.rem(z + d, nz))))
 
-    mean_q, mean_d = front(x_ref, ids_ref, wqkv_ref, wout_ref, wr_ref, blocks, mixed)
+    mean_q, mean_d = front(
+        loads, x_ref, ids_ref, wqkv_ref, wout_ref, wr_ref, blocks, mixed
+    )
+    for step in (-2, -1):
+        loads.wait(len(loads.steps) + step)
 
     pl.semaphore_wait(barrier, nw + nz - 2)
 
@@ -240,63 +283,89 @@
             device_id=peer, device_id_type=MESH,
         )
 
-    def first(d):
-        peer = lax.rem(w + d, nw)
-        return copy(blocks.at[peer], rows.at[z, w], s1.at[d], r1.at[d], (peer, z))
-
-    pltpu.make_async_copy(blocks.at[w], rows.at[z, w], r1.at[0]).start()
-    each(1, nw, lambda d: first(d).start())
+    def first(j):
+        peer = lax.rem(w + STRIDE * j, nw)
+        return copy(blocks.at[peer], rows.at[z, j], s1.at[j], r1.at[j], (peer, z))
+
+    def send_chunk(c):
+        each(jnp.maximum(c * SIZE, 1), (c + 1) * SIZE, lambda j: first(j).start())
 
     def arrived(c):
-        def one(i):
-            origin = c * SIZE + i
-            pltpu.make_async_copy(
-                blocks.at[origin], rows.at[z, origin], r1.at[lax.rem(w - origin + nw, nw)]
-            ).wait()
-
-        each(0, SIZE, one)
-
-    def plane_at(way, hop):
-        return lax.rem(z + nz - hop, nz) if way == 0 else lax.rem(z + hop, nz)
-
-    def move(way, hop, c):
-        block = rows.at[plane_at(way, hop - 1), pl.ds(c * SIZE, SIZE)]
-        return copy(
-            block, block, s2.at[way, hop - 1, c], r2.at[way, hop - 1, c],
-            (w, right if way == 0 else left),
-        )
+        def one(j):
+            pltpu.make_async_copy(blocks.at[j], rows.at[z, j], r1.at[j]).wait()
+
+        each(c * SIZE, (c + 1) * SIZE, one)
+
+    class move:
+        def __init__(self, way, hop, c):
+            plane = lax.rem(z + nz + (2 * way - 1) * (hop - 1), nz)
+            main = rows.at[plane, pl.ds(c * SIZE, SIZE), :, pl.ds(0, D)]
+            self.copies = [
+                copy(
+                    block, block, s2.at[way, hop - 1, c, i], r2.at[way, hop - 1, c, i],
+                    (w, right if way == 0 else left),
+                )
+                for i, block in enumerate((main, sides.at[plane * CHUNKS + c]))
+            ]
+
+        def start(self):
+            for one in self.copies:
+                one.start()
+
+        def wait_recv(self):
+            for one in self.copies:
+                one.wait_recv()
+
+        def wait_send(self):
+            for one in self.copies:
+                one.wait_send()
 
     def work(plane, c):
-        expert_chunk(plane, c, rows, up_ref, turned, extras, slopes, gates, acts)
-
-    def home(c):
+        expert_chunk(plane, c, rows, sides, up_ref, turned, extras, slopes, gates, acts)
+
+    def work_both(hop, c):
+        each(0, 2, lambda way: work(lax.rem(z + nz + (2 * way - 1) * hop, nz), c))
+
+    pltpu.make_async_copy(blocks.at[w], rows.at[z, 0], r1.at[0]).start()
+    for c in range(AHEAD):
+        send_chunk(c)
+
+    def home(c, more):
         arrived(c)
+        sides[z * CHUNKS + c] = pack_side(rows[z, pl.ds(c * SIZE, SIZE), :, D:])
         for way in range(2):
             move(way, 1, c).start()
-        work(z, c)
-
-    each(0, CHUNKS, home)
-
-    def both_ways(hop, c, onward):
+        if more:
+            send_chunk(c + AHEAD)
+
+    each(0, CHUNKS - AHEAD, lambda c: home(c, True))
+    each(CHUNKS - AHEAD, CHUNKS, lambda c: home(c, False))
+
+    def both_ways(hop, c, onward, behind):
         for way in range(2):
             move(way, hop, c).wait_recv()
             if way in onward:
                 move(way, hop + 1, c).start()
-        each(0, 2, lambda way: work(lax.rem(z + nz + (2 * way - 1) * hop, nz), c))
-
-    each(0, (hops - 2) * CHUNKS, lambda i: both_ways(1 + i // CHUNKS, lax.rem(i, CHUNKS), (0, 1)))
-    each(0, CHUNKS // 2, lambda c: both_ways(hops - 1, c, (0,)))
-    each(CHUNKS // 2, CHUNKS, lambda c: both_ways(hops - 1, c, (1,)))
+        behind(c)
+
+    each(0, CHUNKS, lambda c: both_ways(1, c, (0, 1), lambda c: work(z, c)))
+    each(0, (hops - 3) * CHUNKS, lambda i: both_ways(
+        2 + i // CHUNKS, lax.rem(i, CHUNKS), (0, 1), lambda c: work_both(1 + i // CHUNKS, c)
+    ))
+    half_way = CHUNKS // 2
+    each(0, half_way, lambda c: both_ways(hops - 1, c, (0,), lambda c: work_both(hops - 2, c)))
+    each(half_way, CHUNKS, lambda c: both_ways(hops - 1, c, (1,), lambda c: work_both(hops - 2, c)))
+    each(0, CHUNKS, lambda c: work_both(hops - 1, c))
 
     def last(i):
         for way in range(2):
-            move(way, hops, i + way * (CHUNKS // 2)).wait_recv()
-        each(0, 2, lambda way: work(lax.rem(z + hops, nz), i + way * (CHUNKS // 2)))
-
-    each(0, CHUNKS // 2, last)
+            move(way, hops, i + way * half_way).wait_recv()
+        each(0, 2, lambda way: work(lax.rem(z + hops, nz), i + way * half_way))
+
+    each(0, half_way, last)
 
     side = NE // 2 * 16
-    ordered[...] = mm(sequence_order(False), acts[...].reshape(16 * NE, FB)).astype(BF16)
+    ordered[...] = mm(sequence_order(w, False), acts[...].reshape(16 * NE, FB)).astype(BF16)
 
     def partial(which):
         return mm(ordered[pl.ds(pl.multiple_of(which * side, side), side)], down_ref[...])
@@ -357,30 +426,29 @@
     dy = row_gradients(pooled[...].reshape(NE, 16, D).astype(F32), positive_ref[...])
     grad_down_ref[...] = mm(ordered[...], dy, 0, 0)
     back = mm(dy, down_ref[...], 1, 1).astype(BF16)
-    spread[...] = mm(sequence_order(True), back).astype(BF16).reshape(spread.shape)
-
-    def before(q):
-        gate, back = gates[q], spread[q]
-        slope = slopes[q].astype(F32)
-        dpre[q] = (mm(gate[:, :CROWS], back, 0, 0) * slope[:CROWS]).astype(BF16)
-        dpre_x[q] = (
-            mm(gate[:, CROWS : CROWS + MAIN], back, 0, 0) * slope[CROWS:]
-        ).astype(BF16)
-
-    each(0, nz * CHUNKS, before)
+    spread[...] = mm(sequence_order(w, True), back).astype(BF16).reshape(spread.shape)
+
+    grad_up_ref[...] = jnp.zeros_like(grad_up_ref)
+
+    def add(p):
+        left_side, right_side = [], []
+        for c in range(CHUNKS):
+            q = p * CHUNKS + c
+            product = mm(gates[q], spread[q]) * slopes[q].astype(F32)
+            right_side.append(product[:CROWS].astype(BF16))
+            dpre_x[q] = product[CROWS:].astype(BF16)
+            left_side.append(turned[q])
+        grad_up_ref[...] += mm(
+            jnp.concatenate(left_side, axis=1), jnp.concatenate(right_side, axis=0)
+        )
+
+    each(0, nz, add)
     extra_rows = nz * CHUNKS * MAIN
-    grad_up_ref[...] = mm(
+    grad_up_ref[...] += mm(
         extras[...].reshape(extra_rows, D), dpre_x[...].reshape(extra_rows, FB), 0, 0
     )
 
-    def add(p):
-        left_side = jnp.concatenate([turned[p * CHUNKS + c] for c in range(CHUNKS)], axis=1)
-        right_side = dpre[pl.ds(p * CHUNKS, CHUNKS)].reshape(CHUNKS * CROWS, FB)
-        grad_up_ref[...] += mm(left_side, right_side)
-
-    each(0, nz, add)
-
-    each(1, nw, lambda d: first(d).wait_send())
+    each(1, nw, lambda j: first(j).wait_send())
     for way in range(2):
         each(0, (hops - 1) * CHUNKS, lambda i: move(way, 1 + i // CHUNKS, lax.rem(i, CHUNKS)).wait_send())
         each(0, CHUNKS // 2, lambda i: move(way, hops, i + way * (CHUNKS // 2)).wait_send())
@@ -401,19 +469,24 @@
             jax.ShapeDtypeStruct((D, FB), F32),
             jax.ShapeDtypeStruct((FB, D), F32),
         ),
-        in_specs=[vmem] * 8,
+        in_specs=[vmem] * 4 + [pl.BlockSpec(memory_space=pl.ANY)] * 4,
         out_specs=(vmem, vmem),
         scratch_shapes=[
+            pltpu.VMEM(w_qkv.shape, BF16),
+            pltpu.VMEM(w_out.shape, BF16),
+            pltpu.VMEM((D, FB), BF16),
+            pltpu.VMEM((FB, D), BF16),
+            dma((D // 256 + 3, 3)),
             pltpu.VMEM((NE, MAIN, ROW), BF16),
             pltpu.VMEM((TOK, D), BF16),
             pltpu.VMEM((nz, nw, MAIN, ROW), BF16),
+            pltpu.VMEM((parts, SROWS, 128), BF16),
             pltpu.VMEM((parts, D, CROWS), BF16),
             pltpu.VMEM((parts, MAIN, D), BF16),
             pltpu.VMEM((parts, CROWS + MAIN, FB), BF16),
-            pltpu.VMEM((parts, 2 * SIZE, CROWS + 128), BF16),
+            pltpu.VMEM((parts, CROWS + MAIN, 2 * SIZE), BF16),
             pltpu.VMEM((parts, 2 * SIZE, FB), BF16),
             pltpu.VMEM((parts, 2 * SIZE, FB), BF16),
-            pltpu.VMEM((parts, CROWS, FB), BF16),
             pltpu.VMEM((parts, MAIN, FB), BF16),
             pltpu.VMEM((16 * NE, FB), BF16),
             pltpu.VMEM((chips, 16, D), F32),
@@ -424,7 +497,7 @@
             pltpu.VMEM((nz, 16, D), BF16),
             pltpu.VMEM((2, chips, 16, D), BF16),
             dma((nw,)), dma((nw,)),
-            dma((2, nz // 2, CHUNKS)), dma((2, nz // 2, CHUNKS)),
+            dma((2, nz // 2, CHUNKS, 2)), dma((2, nz // 2, CHUNKS, 2)),
             dma((2,)),
             dma((chips,)), dma((chips,)),
             dma((nz,)), dma((nz,)),
@@ -439,9 +512,9 @@
         pair_tokens.reshape(TOK, D),
         expert_ids.reshape(TOK, 2).T,
         positive.reshape(1, -1),
+        w_router.T,
         w_qkv,
         w_out,
-        w_router.T,
         w_up[0],
         w_down[0],
     )

time: 151 us -> 137 us (0.907)
  Pallas kernels: 147 us -> 133 us
    pallas_call x1, Pallas kernels: 147 us -> 133 us  [body(): pl.pallas_call(functools.partial(step_kernel, nw, nz), out_shape=(jax.Sha...]
where the time goes in v3:
time: 137 us
  Pallas kernels  133 us (97%)
  local copies, waits for them, and re-layouts  3.47 us (3%)
    pallas_call x1, Pallas kernels, body(): pl.pallas_call(functools.partial(step_kernel, nw, nz), out_shape=(jax.Sha...  133 us
    unnamed x4, local copies, waits for them, and re-layouts  3.47 us

profile of v3, /device:TPU:1, one launch (start us, length us, event | category | flops | bytes accessed | tf_op | source)
XLA Modules:
  0.0 137.0 jit_solution(3962249989931745258)
XLA Ops:
  0.6 132.9 %contrastive_step.1 = (f32[768,384]{1,0:T(8,128)}, f32[384,768]{1,0:T(8,128)}) custom-call(bf16[256,768]{1,0:T(8,128)(2,1)} %bitcast.14, s32[2,256]{1,0:T(2,128)} %bitcast.16, s32[1,256]{1,0:T(1,128)} %bitcast.17, bf16[32,768]{1,0:T(8,128)(2,1)} %bitcast.15, bf16[768,2304]{1,0:T(8,128)(2,1)} %wqkv_hbm.1, bf16[768,768]{1,0:T(8,128)(2,1)} %wout_hbm.1, ...), custom_call_target="tpu_custom_call" | custom-call | tf_op jit(solution)/shard_map/contrastive_step/pallas_call | solution.py:466
  133.5 0.0 copy-start
  133.5 2.5 %copy.12 = f32[1,768,384]{2,1,0:T(8,128)} copy(f32[1,768,384]{2,1,0:T(8,128)} %bitcast.11) | data formatting | bytes 2359296
  136.0 0.0 copy-done
  136.0 1.0 copy.13
Async XLA Ops:
  133.5 2.5 %copy-start = (f32[384,768]{1,0:T(8,128)S(1)}, f32[384,768]{1,0:T(8,128)}, u32[]{:S(2)}) copy-start(f32[384,768]{1,0:T(8,128)} %get-tuple-element.5) | copy-start | bytes 3538948

commit v4 on v3

--- a/solution.py
+++ b/solution.py
@@ -15,7 +15,6 @@
 MAIN = 16
 ROW = D + 128
 CHUNKS = 4
-AHEAD = 2
 SIZE = NE // CHUNKS
 CROWS = SIZE * MAIN
 SROWS = SIZE * 8
@@ -172,6 +171,17 @@
     return onehot(c == row)
 
 
+def late_rows(w_here, acts, down):
+    pieces, count = D // 128, CHUNKS * 2 * SIZE
+    part = mm(acts.reshape(count, FB), down).astype(BF16)
+    stacked = jnp.concatenate([part[:, k * 128 : (k + 1) * 128] for k in range(pieces)], axis=0)
+    r, c = iota((NE * 16, pieces * count), 0), iota((NE * 16, pieces * count), 1)
+    j = ((w_here + NE - wide_of(r // 16)) * UNSTRIDE) % NE
+    kind, piece = (r % 16) // pieces, (r % 16) % pieces
+    source = piece * count + (j // SIZE) * (2 * SIZE) + kind * SIZE + j % SIZE
+    return mm(onehot((c == source) & (kind < 2)), stacked).reshape(2, NE // 2, 16, 128)
+
+
 def split(v):
     high = v.astype(BF16)
     return high, (v - high.astype(F32)).astype(BF16)
@@ -223,8 +233,8 @@
     grad_up_ref, grad_down_ref,
     wqkv_ref, wout_ref, up_ref, down_ref, load_sems,
     blocks, mixed, rows, sides, turned, extras, slopes, gates, acts, spread, dpre_x,
-    ordered, part, lent, half, got, zsend, zgot, pooled,
-    s1, r1, s2, r2, sem_core, s3, r3, s4, r4, s5, r5, s6, r6,
+    ordered, part, lent, half, got, late_all, late_lent, late_half, late_send, late_got, zsend, zgot, pooled,
+    s1, r1, s2, r2, sem_core, s3, r3, s4, r4, s5, r5, s6, r6, s7, r7,
 ):
     w, z = lax.axis_index("wide"), lax.axis_index("narrow")
     right, left = lax.rem(z + 1, nz), lax.rem(z + nz - 1, nz)
@@ -290,22 +300,33 @@
     def send_chunk(c):
         each(jnp.maximum(c * SIZE, 1), (c + 1) * SIZE, lambda j: first(j).start())
 
+    def onward(way, j):
+        block = rows.at[z, j, :, pl.ds(0, D)]
+        c = j // SIZE
+        return copy(
+            block, block, s2.at[way, 0, c, 0], r2.at[way, 0, c, 0],
+            (w, right if way == 0 else left),
+        )
+
     def arrived(c):
         def one(j):
             pltpu.make_async_copy(blocks.at[j], rows.at[z, j], r1.at[j]).wait()
+            for way in range(2):
+                onward(way, j).start()
 
         each(c * SIZE, (c + 1) * SIZE, one)
 
     class move:
-        def __init__(self, way, hop, c):
+        def __init__(self, way, hop, c, items=(0, 1)):
             plane = lax.rem(z + nz + (2 * way - 1) * (hop - 1), nz)
             main = rows.at[plane, pl.ds(c * SIZE, SIZE), :, pl.ds(0, D)]
+            blocks = (main, sides.at[plane * CHUNKS + c])
             self.copies = [
                 copy(
-                    block, block, s2.at[way, hop - 1, c, i], r2.at[way, hop - 1, c, i],
+                    blocks[i], blocks[i], s2.at[way, hop - 1, c, i], r2.at[way, hop - 1, c, i],
                     (w, right if way == 0 else left),
                 )
-                for i, block in enumerate((main, sides.at[plane * CHUNKS + c]))
+                for i in items
             ]
 
         def start(self):
@@ -327,19 +348,15 @@
         each(0, 2, lambda way: work(lax.rem(z + nz + (2 * way - 1) * hop, nz), c))
 
     pltpu.make_async_copy(blocks.at[w], rows.at[z, 0], r1.at[0]).start()
-    for c in range(AHEAD):
-        send_chunk(c)
-
-    def home(c, more):
+    each(0, CHUNKS, send_chunk)
+
+    def home(c):
         arrived(c)
         sides[z * CHUNKS + c] = pack_side(rows[z, pl.ds(c * SIZE, SIZE), :, D:])
         for way in range(2):
-            move(way, 1, c).start()
-        if more:
-            send_chunk(c + AHEAD)
-
-    each(0, CHUNKS - AHEAD, lambda c: home(c, True))
-    each(CHUNKS - AHEAD, CHUNKS, lambda c: home(c, False))
+            move(way, 1, c, (1,)).start()
+
+    each(0, CHUNKS, home)
 
     def both_ways(hop, c, onward, behind):
         for way in range(2):
@@ -357,13 +374,8 @@
     each(half_way, CHUNKS, lambda c: both_ways(hops - 1, c, (1,), lambda c: work_both(hops - 2, c)))
     each(0, CHUNKS, lambda c: work_both(hops - 1, c))
 
-    def last(i):
-        for way in range(2):
-            move(way, hops, i + way * half_way).wait_recv()
-        each(0, 2, lambda way: work(lax.rem(z + hops, nz), i + way * half_way))
-
-    each(0, half_way, last)
-
+    far = lax.rem(z + hops, nz)
+    acts[pl.ds(far * CHUNKS, CHUNKS)] = jnp.zeros((CHUNKS, 2 * SIZE, FB), BF16)
     side = NE // 2 * 16
     ordered[...] = mm(sequence_order(w, False), acts[...].reshape(16 * NE, FB)).astype(BF16)
 
@@ -398,6 +410,15 @@
         block = pooled.at[holder, origin]
         return copy(block, block, s6.at[d], r6.at[d], (sibling, z))
 
+    each(1, chips, lambda d: scatter(d).start())
+
+    def last(i):
+        for way in range(2):
+            move(way, hops, i + way * half_way).wait_recv()
+        each(0, 2, lambda way: work(lax.rem(z + hops, nz), i + way * half_way))
+
+    each(0, half_way, last)
+
     def summed(count, one_copy, buffer, start):
         def one(d, total):
             one_copy(d).wait_recv()
@@ -405,12 +426,39 @@
 
         return lax.fori_loop(1, count, one, start)
 
-    each(1, chips, lambda d: scatter(d).start())
-    total = summed(chips, scatter, got, part[chip]) * (1.0 / SEQ)
+    late_all[...] = late_rows(w, acts[pl.ds(far * CHUNKS, CHUNKS)], down_ref[...])
+    late_lent[...] = late_all[1 - core].astype(BF16)
+    late_swap = copy(late_lent, late_half, sem_core.at[2], sem_core.at[3], (sibling, z))
+    late_swap.start()
+    late_swap.wait_recv()
+    late_part = late_all[core] + late_half[...].astype(F32)
+    late_all[core] = late_part
+    late_send[...] = late_part.astype(BF16)
+
+    def late_scatter(d):
+        return copy(
+            late_send.at[peer_chip(d)], late_got.at[d], s7.at[d], r7.at[d],
+            (peer_chip(d) * 2 + core, z),
+        )
+
+    each(1, chips, lambda d: late_scatter(d).start())
+    total = summed(chips, scatter, got, part[chip])
+    late = summed(chips, late_scatter, late_got, late_all[core, chip])
     row = iota((16, 1), 0)
+    pieces = D // 128
+    total = total + jnp.concatenate(
+        [
+            jnp.where(row == far, late[k : k + 1], 0.0)
+            + jnp.where(row == far + 8, late[pieces + k : pieces + k + 1], 0.0)
+            for k in range(pieces)
+        ],
+        axis=1,
+    )
+    total = total * (1.0 / SEQ)
     total = total + jnp.where(row == z, mean_q, 0.0) + jnp.where(row == z + 8, mean_d, 0.0)
     zsend[...] = total.astype(BF16)
     each(1, nz, lambda d: across(d).start())
+    ordered[...] = mm(sequence_order(w, False), acts[...].reshape(16 * NE, FB)).astype(BF16)
     pooled[core, chip] = summed(nz, across, zgot, total).astype(BF16)
     each(1, chips, lambda d: gather(d, chip).start())
     lend(0, chip, core).start()
@@ -453,6 +501,8 @@
         each(0, (hops - 1) * CHUNKS, lambda i: move(way, 1 + i // CHUNKS, lax.rem(i, CHUNKS)).wait_send())
         each(0, CHUNKS // 2, lambda i: move(way, hops, i + way * (CHUNKS // 2)).wait_send())
     each(1, chips, lambda d: scatter(d).wait_send())
+    late_swap.wait_send()
+    each(1, chips, lambda d: late_scatter(d).wait_send())
     each(1, nz, lambda d: across(d).wait_send())
     each(1, chips, lambda d: gather(d, chip).wait_send())
     each(0, chips, lambda d: lend(d, lax.rem(chip - d + chips, chips), core).wait_send())
@@ -493,14 +543,20 @@
             pltpu.VMEM((chips, 16, D), BF16),
             pltpu.VMEM((chips, 16, D), BF16),
             pltpu.VMEM((chips, 16, D), BF16),
+            pltpu.VMEM((2, chips, 16, 128), F32),
+            pltpu.VMEM((chips, 16, 128), BF16),
+            pltpu.VMEM((chips, 16, 128), BF16),
+            pltpu.VMEM((chips, 16, 128), BF16),
+            pltpu.VMEM((chips, 16, 128), BF16),
             pltpu.VMEM((16, D), BF16),
             pltpu.VMEM((nz, 16, D), BF16),
             pltpu.VMEM((2, chips, 16, D), BF16),
             dma((nw,)), dma((nw,)),
             dma((2, nz // 2, CHUNKS, 2)), dma((2, nz // 2, CHUNKS, 2)),
-            dma((2,)),
+            dma((4,)),
             dma((chips,)), dma((chips,)),
             dma((nz,)), dma((nz,)),
+            dma((chips,)), dma((chips,)),
             dma((chips,)), dma((chips,)),
             dma((chips,)), dma((chips,)),
         ],

time: 137 us -> 131 us (0.956)
  Pallas kernels: 133 us -> 127 us
    pallas_call x1, Pallas kernels: 133 us -> 127 us  [body(): pl.pallas_call(functools.partial(step_kernel, nw, nz), out_shape=(jax.Sha...]
where the time goes in v4:
time: 131 us
  Pallas kernels  127 us (97%)
  local copies, waits for them, and re-layouts  3.47 us (3%)
    pallas_call x1, Pallas kernels, body(): pl.pallas_call(functools.partial(step_kernel, nw, nz), out_shape=(jax.Sha...  127 us
    unnamed x4, local copies, waits for them, and re-layouts  3.47 us

profile of v4, /device:TPU:1, one launch (start us, length us, event | category | flops | bytes accessed | tf_op | source)
XLA Modules:
  0.0 131.2 jit_solution(5428302090473902040)
XLA Ops:
  0.6 127.0 %contrastive_step.1 = (f32[768,384]{1,0:T(8,128)}, f32[384,768]{1,0:T(8,128)}) custom-call(bf16[256,768]{1,0:T(8,128)(2,1)} %bitcast.14, s32[2,256]{1,0:T(2,128)} %bitcast.16, s32[1,256]{1,0:T(1,128)} %bitcast.17, bf16[32,768]{1,0:T(8,128)(2,1)} %bitcast.15, bf16[768,2304]{1,0:T(8,128)(2,1)} %wqkv_hbm.1, bf16[768,768]{1,0:T(8,128)(2,1)} %wout_hbm.1, ...), custom_call_target="tpu_custom_call" | custom-call | tf_op jit(solution)/shard_map/contrastive_step/pallas_call | solution.py:516
  127.7 0.0 copy-start
  127.7 2.5 %copy.12 = f32[1,768,384]{2,1,0:T(8,128)} copy(f32[1,768,384]{2,1,0:T(8,128)} %bitcast.11) | data formatting | bytes 2359296
  130.1 0.0 copy-done
  130.1 1.0 copy.13
Async XLA Ops:
  127.7 2.5 %copy-start = (f32[384,768]{1,0:T(8,128)S(1)}, f32[384,768]{1,0:T(8,128)}, u32[]{:S(2)}) copy-start(f32[384,768]{1,0:T(8,128)} %get-tuple-element.5) | copy-start | bytes 3538948

commit v5 on v4

--- a/solution.py
+++ b/solution.py
@@ -171,15 +171,20 @@
     return onehot(c == row)
 
 
-def late_rows(w_here, acts, down):
+def late_order(w_here):
     pieces, count = D // 128, CHUNKS * 2 * SIZE
-    part = mm(acts.reshape(count, FB), down).astype(BF16)
-    stacked = jnp.concatenate([part[:, k * 128 : (k + 1) * 128] for k in range(pieces)], axis=0)
     r, c = iota((NE * 16, pieces * count), 0), iota((NE * 16, pieces * count), 1)
     j = ((w_here + NE - wide_of(r // 16)) * UNSTRIDE) % NE
     kind, piece = (r % 16) // pieces, (r % 16) % pieces
     source = piece * count + (j // SIZE) * (2 * SIZE) + kind * SIZE + j % SIZE
-    return mm(onehot((c == source) & (kind < 2)), stacked).reshape(2, NE // 2, 16, 128)
+    return onehot((c == source) & (kind < 2))
+
+
+def late_rows(order, acts, down):
+    pieces, count = D // 128, CHUNKS * 2 * SIZE
+    part = mm(acts.reshape(count, FB), down).astype(BF16)
+    stacked = jnp.concatenate([part[:, k * 128 : (k + 1) * 128] for k in range(pieces)], axis=0)
+    return mm(order, stacked).reshape(2, NE // 2, 16, 128)
 
 
 def split(v):
@@ -187,7 +192,17 @@
     return high, (v - high.astype(F32)).astype(BF16)
 
 
-def row_gradients(pooled, positive):
+def targets(positive):
+    pairs = 8 * NE
+
+    def number(j):
+        return wide_of(j // 8) * 8 + j % 8
+
+    r, c = iota((pairs, pairs), 0), iota((pairs, pairs), 1)
+    return mm(onehot(number(r) == c), onehot(number(r) == positive), 1, 1)
+
+
+def row_gradients(pooled, target):
     pairs = 8 * NE
     query = pooled[:, :8].reshape(pairs, D)
     document = pooled[:, 8:].reshape(pairs, D)
@@ -199,11 +214,6 @@
     weights = jnp.exp(mm(query_b, document_b, 1, 1) * (inverse_q * WARMTH) * inverse_row)
     probs = weights / jnp.sum(weights, axis=1, keepdims=True)
 
-    def number(j):
-        return wide_of(j // 8) * 8 + j % 8
-
-    r, c = iota((pairs, pairs), 0), iota((pairs, pairs), 1)
-    target = mm(onehot(number(r) == c), onehot(number(r) == positive), 1, 1)
     excess = (probs - target) * (LOSS_SCALE * WARMTH)
     high, rest = split(excess * inverse_row)
     grad_q = mm(high, document_b) + mm(rest, document_b)
@@ -233,7 +243,7 @@
     grad_up_ref, grad_down_ref,
     wqkv_ref, wout_ref, up_ref, down_ref, load_sems,
     blocks, mixed, rows, sides, turned, extras, slopes, gates, acts, spread, dpre_x,
-    ordered, part, lent, half, got, late_all, late_lent, late_half, late_send, late_got, zsend, zgot, pooled,
+    order, order_back, order_late, target, ordered, part, lent, half, got, late_all, late_lent, late_half, late_send, late_got, zsend, zgot, pooled,
     s1, r1, s2, r2, sem_core, s3, r3, s4, r4, s5, r5, s6, r6, s7, r7,
 ):
     w, z = lax.axis_index("wide"), lax.axis_index("narrow")
@@ -358,6 +368,11 @@
 
     each(0, CHUNKS, home)
 
+    order[...] = sequence_order(w, False)
+    order_back[...] = sequence_order(w, True)
+    order_late[...] = late_order(w)
+    target[...] = targets(positive_ref[...])
+
     def both_ways(hop, c, onward, behind):
         for way in range(2):
             move(way, hop, c).wait_recv()
@@ -377,7 +392,7 @@
     far = lax.rem(z + hops, nz)
     acts[pl.ds(far * CHUNKS, CHUNKS)] = jnp.zeros((CHUNKS, 2 * SIZE, FB), BF16)
     side = NE // 2 * 16
-    ordered[...] = mm(sequence_order(w, False), acts[...].reshape(16 * NE, FB)).astype(BF16)
+    ordered[...] = mm(order[...], acts[...].reshape(16 * NE, FB)).astype(BF16)
 
     def partial(which):
         return mm(ordered[pl.ds(pl.multiple_of(which * side, side), side)], down_ref[...])
@@ -415,7 +430,8 @@
     def last(i):
         for way in range(2):
             move(way, hops, i + way * half_way).wait_recv()
-        each(0, 2, lambda way: work(lax.rem(z + hops, nz), i + way * half_way))
+        for way in range(2):
+            work(lax.rem(z + hops, nz), i + way * half_way)
 
     each(0, half_way, last)
 
@@ -426,7 +442,7 @@
 
         return lax.fori_loop(1, count, one, start)
 
-    late_all[...] = late_rows(w, acts[pl.ds(far * CHUNKS, CHUNKS)], down_ref[...])
+    late_all[...] = late_rows(order_late[...], acts[pl.ds(far * CHUNKS, CHUNKS)], down_ref[...])
     late_lent[...] = late_all[1 - core].astype(BF16)
     late_swap = copy(late_lent, late_half, sem_core.at[2], sem_core.at[3], (sibling, z))
     late_swap.start()
@@ -458,7 +474,7 @@
     total = total + jnp.where(row == z, mean_q, 0.0) + jnp.where(row == z + 8, mean_d, 0.0)
     zsend[...] = total.astype(BF16)
     each(1, nz, lambda d: across(d).start())
-    ordered[...] = mm(sequence_order(w, False), acts[...].reshape(16 * NE, FB)).astype(BF16)
+    ordered[...] = mm(order[...], acts[...].reshape(16 * NE, FB)).astype(BF16)
     pooled[core, chip] = summed(nz, across, zgot, total).astype(BF16)
     each(1, chips, lambda d: gather(d, chip).start())
     lend(0, chip, core).start()
@@ -471,10 +487,10 @@
     each(1, chips, pass_on)
     each(0, chips, lambda d: lend(d, lax.rem(chip - d + chips, chips), 1 - core).wait_recv())
 
-    dy = row_gradients(pooled[...].reshape(NE, 16, D).astype(F32), positive_ref[...])
+    dy = row_gradients(pooled[...].reshape(NE, 16, D).astype(F32), target[...])
     grad_down_ref[...] = mm(ordered[...], dy, 0, 0)
     back = mm(dy, down_ref[...], 1, 1).astype(BF16)
-    spread[...] = mm(sequence_order(w, True), back).astype(BF16).reshape(spread.shape)
+    spread[...] = mm(order_back[...], back).astype(BF16).reshape(spread.shape)
 
     grad_up_ref[...] = jnp.zeros_like(grad_up_ref)
 
@@ -538,6 +554,10 @@
             pltpu.VMEM((parts, 2 * SIZE, FB), BF16),
             pltpu.VMEM((parts, 2 * SIZE, FB), BF16),
             pltpu.VMEM((parts, MAIN, FB), BF16),
+            pltpu.VMEM((16 * NE, 16 * NE), BF16),
+            pltpu.VMEM((16 * NE, 16 * NE), BF16),
+            pltpu.VMEM((16 * NE, D // 128 * CHUNKS * 2 * SIZE), BF16),
+            pltpu.VMEM((8 * NE, 8 * NE), F32),
             pltpu.VMEM((16 * NE, FB), BF16),
             pltpu.VMEM((chips, 16, D), F32),
             pltpu.VMEM((chips, 16, D), BF16),

time: 131 us -> 131 us (level)
  no operation moved by 1% of the time
where the time goes in v5:
time: 131 us
  Pallas kernels  127 us (97%)
  local copies, waits for them, and re-layouts  3.47 us (3%)
    pallas_call x1, Pallas kernels, body(): pl.pallas_call(functools.partial(step_kernel, nw, nz), out_shape=(jax.Sha...  127 us
    unnamed x4, local copies, waits for them, and re-layouts  3.47 us

profile of v5, /device:TPU:1, one launch (start us, length us, event | category | flops | bytes accessed | tf_op | source)
XLA Modules:
  0.0 130.9 jit_solution(5116214786006620979)
XLA Ops:
  0.6 126.7 %contrastive_step.1 = (f32[768,384]{1,0:T(8,128)}, f32[384,768]{1,0:T(8,128)}) custom-call(bf16[256,768]{1,0:T(8,128)(2,1)} %bitcast.14, s32[2,256]{1,0:T(2,128)} %bitcast.16, s32[1,256]{1,0:T(1,128)} %bitcast.17, bf16[32,768]{1,0:T(8,128)(2,1)} %bitcast.15, bf16[768,2304]{1,0:T(8,128)(2,1)} %wqkv_hbm.1, bf16[768,768]{1,0:T(8,128)(2,1)} %wout_hbm.1, ...), custom_call_target="tpu_custom_call" | custom-call | tf_op jit(solution)/shard_map/contrastive_step/pallas_call | solution.py:532
  127.4 0.0 copy-start
  127.4 2.5 %copy.12 = f32[1,768,384]{2,1,0:T(8,128)} copy(f32[1,768,384]{2,1,0:T(8,128)} %bitcast.11) | data formatting | bytes 2359296
  129.9 0.0 copy-done
  129.9 1.0 copy.13
Async XLA Ops:
  127.4 2.5 %copy-start = (f32[384,768]{1,0:T(8,128)S(1)}, f32[384,768]{1,0:T(8,128)}, u32[]{:S(2)}) copy-start(f32[384,768]{1,0:T(8,128)} %get-tuple-element.5) | copy-start | bytes 3538948

commit v6 on v5

--- a/solution.py
+++ b/solution.py
@@ -243,7 +243,7 @@
     grad_up_ref, grad_down_ref,
     wqkv_ref, wout_ref, up_ref, down_ref, load_sems,
     blocks, mixed, rows, sides, turned, extras, slopes, gates, acts, spread, dpre_x,
-    order, order_back, order_late, target, ordered, part, lent, half, got, late_all, late_lent, late_half, late_send, late_got, zsend, zgot, pooled,
+    order, order_back, order_late, target, turned_acts, turned_extras, ordered, part, lent, half, got, late_all, late_lent, late_half, late_send, late_got, zsend, zgot, pooled,
     s1, r1, s2, r2, sem_core, s3, r3, s4, r4, s5, r5, s6, r6, s7, r7,
 ):
     w, z = lax.axis_index("wide"), lax.axis_index("narrow")
@@ -474,7 +474,8 @@
     total = total + jnp.where(row == z, mean_q, 0.0) + jnp.where(row == z + 8, mean_d, 0.0)
     zsend[...] = total.astype(BF16)
     each(1, nz, lambda d: across(d).start())
-    ordered[...] = mm(order[...], acts[...].reshape(16 * NE, FB)).astype(BF16)
+    turned_acts[...] = mm(order[...], acts[...].reshape(16 * NE, FB)).astype(BF16).T
+    turned_extras[...] = extras[...].reshape(turned_extras.shape[1], D).T
     pooled[core, chip] = summed(nz, across, zgot, total).astype(BF16)
     each(1, chips, lambda d: gather(d, chip).start())
     lend(0, chip, core).start()
@@ -488,7 +489,7 @@
     each(0, chips, lambda d: lend(d, lax.rem(chip - d + chips, chips), 1 - core).wait_recv())
 
     dy = row_gradients(pooled[...].reshape(NE, 16, D).astype(F32), target[...])
-    grad_down_ref[...] = mm(ordered[...], dy, 0, 0)
+    grad_down_ref[...] = mm(turned_acts[...], dy)
     back = mm(dy, down_ref[...], 1, 1).astype(BF16)
     spread[...] = mm(order_back[...], back).astype(BF16).reshape(spread.shape)
 
@@ -509,7 +510,7 @@
     each(0, nz, add)
     extra_rows = nz * CHUNKS * MAIN
     grad_up_ref[...] += mm(
-        extras[...].reshape(extra_rows, D), dpre_x[...].reshape(extra_rows, FB), 0, 0
+        turned_extras[...], dpre_x[...].reshape(extra_rows, FB)
     )
 
     each(1, nw, lambda j: first(j).wait_send())
@@ -558,6 +559,8 @@
             pltpu.VMEM((16 * NE, 16 * NE), BF16),
             pltpu.VMEM((16 * NE, D // 128 * CHUNKS * 2 * SIZE), BF16),
             pltpu.VMEM((8 * NE, 8 * NE), F32),
+            pltpu.VMEM((FB, 16 * NE), BF16),
+            pltpu.VMEM((D, parts * MAIN), BF16),
             pltpu.VMEM((16 * NE, FB), BF16),
             pltpu.VMEM((chips, 16, D), F32),
             pltpu.VMEM((chips, 16, D), BF16),

time: 131 us -> 131 us (level)
  no operation moved by 1% of the time
where the time goes in v6:
time: 131 us
  Pallas kernels  127 us (97%)
  local copies, waits for them, and re-layouts  3.47 us (3%)
    pallas_call x1, Pallas kernels, body(): pl.pallas_call(functools.partial(step_kernel, nw, nz), out_shape=(jax.Sha...  127 us
    unnamed x4, local copies, waits for them, and re-layouts  3.47 us

profile of v6, /device:TPU:1, one launch (start us, length us, event | category | flops | bytes accessed | tf_op | source)
XLA Modules:
  0.0 130.9 jit_solution(2181416304888905771)
XLA Ops:
  0.6 126.8 %contrastive_step.1 = (f32[768,384]{1,0:T(8,128)}, f32[384,768]{1,0:T(8,128)}) custom-call(bf16[256,768]{1,0:T(8,128)(2,1)} %bitcast.14, s32[2,256]{1,0:T(2,128)} %bitcast.16, s32[1,256]{1,0:T(1,128)} %bitcast.17, bf16[32,768]{1,0:T(8,128)(2,1)} %bitcast.15, bf16[768,2304]{1,0:T(8,128)(2,1)} %wqkv_hbm.1, bf16[768,768]{1,0:T(8,128)(2,1)} %wout_hbm.1, ...), custom_call_target="tpu_custom_call" | custom-call | tf_op jit(solution)/shard_map/contrastive_step/pallas_call | solution.py:533
  127.4 0.0 copy-start
  127.4 2.5 %copy.12 = f32[1,768,384]{2,1,0:T(8,128)} copy(f32[1,768,384]{2,1,0:T(8,128)} %bitcast.11) | data formatting | bytes 2359296
  129.9 0.0 copy-done
  129.9 1.0 copy.13
Async XLA Ops:
  127.4 2.5 %copy-start = (f32[384,768]{1,0:T(8,128)S(1)}, f32[384,768]{1,0:T(8,128)}, u32[]{:S(2)}) copy-start(f32[384,768]{1,0:T(8,128)} %get-tuple-element.5) | copy-start | bytes 3538948
